TPU v7x, 128 devices: a whole 4x4x4 slice. The times are simulated.
128 devices in a mesh: rep: 2 (over x_lo), row: 16 (over z, x_hi, core), col: 4 (over y).
Axes of the slice: x: 4 (x_hi: 2, x_lo: 2; x = x_hi * 2 + x_lo), y: 4, z: 4, core: 2. Of those that a mesh axis runs over, the one named last changes fastest.
Arguments:
- tokens: bfloat16 [1024, 8192], P(('rep', 'row'), 'col'), may hold values from -6 to 6
- probe_bits: int32 [1024, 8192], P('rep', 'col'), may hold values from 0 to 1
- cot_codes: int32 [1024, 8192], P('rep', 'col'), may hold values from 40 to 207, as said below
- cot_scales: int32 [1024, 256], P('rep', 'col'), may hold values from -2 to 2
- w_gate: bfloat16 [8192, 14336], P('col', 'row'), may hold values from -0.0625 to 0.0625
- w_up: bfloat16 [8192, 14336], P('col', 'row'), may hold values from -0.0625 to 0.0625
- w_down: bfloat16 [14336, 8192], P('row', 'col'), may hold values from -0.046875 to 0.046875
Outputs:
- grad_out: bfloat16 [1024, 8192], P(('rep', 'row'), 'col')
- hess_out: bfloat16 [1024, 8192], P(('rep', 'row'), 'col')
- diag_out: float32 [8192], P('col')
Inputs may be any that keep to these rules, and one draw needn't show every extreme that they name: `cot_codes`: each code is an E4M3 byte: sign in bit 7, exponent field (bits 3 to 6) from 5 to 9, mantissa in bits 0 to 2.
All inputs are finite; a program needn't handle non-finite values.
Results may differ from a plain program's by a relative error of at most 0.019.
Values may be sent and summed in bfloat16 or wider, within the bound.
A program may use at most 128 MiB of HBM per device.

v0:
```python
import jax
import jax.numpy as jnp
from jax import lax
from jax.sharding import PartitionSpec as P


def power_two(exponent):
    result = jnp.zeros(exponent.shape, jnp.float32)
    for level in range(-4, 5):
        result = jnp.where(exponent == level, jnp.float32(2.0**level), result)
    return result


def decode(code_vals, scale_exp):
    sign_val = (1 - 2 * (code_vals // 128)).astype(jnp.float32)
    field = code_vals // 8 % 16
    mantissa = (code_vals % 8).astype(jnp.float32)
    expanded = jnp.repeat(scale_exp, 32, axis=1)
    return sign_val * (1.0 + mantissa / 8.0) * power_two(field - 7 + expanded)


def local_terms(gate_pre, up_pre, gate_tan, up_tan, down_back):
    sig_gate = jax.nn.sigmoid(gate_pre)
    first_der = sig_gate * (1.0 + gate_pre * (1.0 - sig_gate))
    second_der = sig_gate * (1.0 - sig_gate) * (2.0 + gate_pre * (1.0 - 2.0 * sig_gate))
    term_a = down_back * up_pre * first_der
    term_b = down_back * gate_pre * sig_gate
    term_c = down_back * (up_tan * first_der + up_pre * second_der * gate_tan)
    term_d = down_back * first_der * gate_tan
    return jnp.stack([term_a, term_b, term_c, term_d]).astype(jnp.bfloat16)


def transposed(left, weight):
    return lax.dot_general(
        left, weight, (((1,), (1,)), ((), ())), preferred_element_type=jnp.float32
    )


def local(tokens, probe_bits, cot_codes, cot_scales, w_gate, w_up, w_down):
    hidden_cols = w_gate.shape[1]
    feat_cols = tokens.shape[1]
    own_rows = tokens.shape[0]
    signs = (2 * probe_bits - 1).astype(jnp.bfloat16)
    cotangent = decode(cot_codes, cot_scales).astype(jnp.bfloat16)
    block_rows = lax.all_gather(tokens, "row", axis=0, tiled=True)
    gate_part = jnp.dot(block_rows, w_gate, preferred_element_type=jnp.float32)
    up_part = jnp.dot(block_rows, w_up, preferred_element_type=jnp.float32)
    primal = jnp.concatenate([gate_part, up_part], axis=1)
    gate_pre = primal[:, :hidden_cols]
    up_pre = primal[:, hidden_cols:]
    gate_tan = jnp.dot(signs, w_gate, preferred_element_type=jnp.float32)
    up_tan = jnp.dot(signs, w_up, preferred_element_type=jnp.float32)
    down_back = transposed(cotangent, w_down)
    reduced = lax.psum((gate_pre, up_pre, gate_tan, up_tan, down_back), "col")
    stacked = local_terms(*reduced)
    grad_term = transposed(stacked[0], w_gate) + transposed(stacked[1], w_up)
    hess_term = transposed(stacked[2], w_gate) + transposed(stacked[3], w_up)
    combined = lax.psum_scatter(
        jnp.concatenate([grad_term, hess_term], axis=1).astype(jnp.bfloat16),
        "row",
        scatter_dimension=0,
        tiled=True,
    ).astype(jnp.float32)
    grad_full = combined[:, :feat_cols]
    hess_full = combined[:, feat_cols:]
    offset = lax.axis_index("row") * own_rows
    own_bits = lax.dynamic_slice_in_dim(probe_bits, offset, own_rows, 0)
    own_signs = (2 * own_bits - 1).astype(jnp.float32)
    partial_value = jnp.sum(own_signs * hess_full, axis=0)
    summed = lax.psum(partial_value, ("rep", "row"))
    total_tokens = own_rows * lax.axis_size("row") * lax.axis_size("rep")
    diag_out = summed / jnp.float32(total_tokens)
    return (grad_full.astype(jnp.bfloat16), hess_full.astype(jnp.bfloat16), diag_out)


def solution(mesh):
    in_specs = (
        P(("rep", "row"), "col"),
        P("rep", "col"),
        P("rep", "col"),
        P("rep", "col"),
        P("col", "row"),
        P("col", "row"),
        P("row", "col"),
    )
    out_specs = (P(("rep", "row"), "col"), P(("rep", "row"), "col"), P("col"))
    return jax.shard_map(local, mesh=mesh, in_specs=in_specs, out_specs=out_specs, check_vma=False)
```

profile of v0, /device:TPU:0, one launch (start us, length us, event | category | flops | bytes accessed | tf_op | source)
XLA Modules:
  0.0 417.8 jit_solution(1173214333366789003)
XLA Ops:
  7.2 0.7 all-gather.2.cloned.1.call-update
  7.9 5.4 %copy.15 = s32[512,2048]{0,1:T(8,128)} copy(s32[512,2048]{1,0:T(8,128)} %param.8) | data formatting | bytes 8388608 | tf_op args[1]
  13.3 5.5 %copy.11 = s32[512,2048]{0,1:T(8,128)} copy(s32[512,2048]{1,0:T(8,128)} %param.9) | data formatting | bytes 8388608 | tf_op args[2]
  18.8 12.0 %fusion.6 = bf16[512,2048]{0,1:T(8,128)(2,1)S(1)} fusion(s32[512,2048]{0,1:T(8,128)} %copy.11, s32[512,64]{0,1:T(8,128)S(1)} %copy-done.1), kind=kLoop, calls=%fused_computation.17 | loop fusion | flops 72351744 | bytes 6422528 | tf_op jit(solution)/shard_map/convert_element_type | solution.py:44
  30.8 3.7 fusion.41
  34.5 3.6 fusion.29
  38.1 3.6 fusion.30
  41.7 18.9 %all-gather.2.cloned.1.call-done = bf16[512,2048]{1,0:T(8,128)(2,1)} async-done(((bf16[32,2048]{1,0:T(8,128)(2,1)}), bf16[512,2048]{1,0:T(8,128)(2,1)}) %all-gather.2.cloned.1.call-update) | async-done | bytes 2097168 | tf_op jit(solution)/shard_map/all_gather | solution.py:45
  60.6 6.4 %fusion.42 = f32[512,896]{1,0:T(8,128)} fusion(bf16[512,2048]{1,0:T(8,128)(2,1)} %all-gather.2.cloned.1.call-done, bf16[2048,896]{1,0:T(8,128)(2,1)} %param.12), kind=kOutput, calls=%fused_computation.62 | convolution fusion | flops 1879048192 | bytes 7602176 | tf_op jit(solution)/shard_map/dot_general | solution.py:47
  67.0 3.6 fusion.43
  70.6 0.2 reduce-scatter.2.cloned.1.call-start
  70.8 173.0 %all-reduce.3.cloned.1.call-done = (f32[512,896]{1,0:T(8,128)}, f32[512,896]{1,0:T(8,128)}, f32[512,896]{1,0:T(8,128)}, f32[512,896]{1,0:T(8,128)}, f32[512,896]{1,0:T(8,128)}) async-done(((f32[512,896]{1,0:T(8,128)}, f32[512,896]{1,0:T(8,128)}, f32[512,896]{1,0:T(8,128)}, f32[512,896]{1,0:T(8,128)}, f32[512,896]{1,0:T(8,128)}), (f32[512,896]{1,0:T(8,128)}, f32[512,896]{1,0:T(8,128)}, f32[512,896]{1,0:T(8,128)}, ...) | async-done | bytes 9175056 | tf_op jit(solution)/shard_map/psum | solution.py:54
  243.9 6.4 %fusion.23 = f32[512,2048]{1,0:T(8,128)S(1)} fusion(bf16[2048,896]{1,0:T(8,128)(2,1)} %param.11, f32[512,896]{1,0:T(8,128)} %get-tuple-element.3, f32[512,896]{1,0:T(8,128)} %get-tuple-element.5, f32[512,896]{1,0:T(8,128)} %get-tuple-element.6), kind=kOutput, calls=%fused_computation.45 | convolution fusion | flops 1883635712 | bytes 13369344 | tf_op jit(solution)/shard_map/dot_general | solution.py:34
  250.3 2.4 add_convert_fusion.2
  252.9 0.5 copy-done.12
  253.5 0.5 copy-done.13
  254.0 3.1 fusion.24
  257.1 2.8 add_convert_fusion
  259.9 2.4 pad_maximum_fusion
  262.4 80.7 %reduce-scatter.2.cloned.1.call-done = bf16[32,4096]{1,0:T(8,128)(2,1)} async-done(((bf16[512,4096]{1,0:T(8,128)(2,1)}), bf16[32,4096]{1,0:T(8,128)(2,1)}) %reduce-scatter.2.cloned.1.call-update) | async-done | bytes 262160 | tf_op jit(solution)/shard_map/reduce_scatter | solution.py:58
  343.1 1.7 multiply_reduce_fusion
  344.8 64.4 %psum.47 = f32[2048]{0:T(1024)S(1)} all-reduce(f32[2048]{0:T(1024)S(1)} %get-tuple-element.8), channel_id=1, replica_groups=mesh['rep'=2,'row'=16,'col'=4] {'rep','row'}, use_global_device_ids=true, to_apply=%region_7.8 | all-reduce | flops 2048 | bytes 16384 | tf_op jit(solution)/shard_map/psum | solution.py:70
  409.1 0.6 broadcast_multiply_fusion
  409.7 1.6 slice.17
  (30 shorter events, 0.3 us)
Async XLA Ops:
  7.2 53.4 %all-gather.2.cloned.1.call-start = ((), (), s32[]{:S(2)}) async-start(), calls=%async_computation.1 | async-start | bytes 2228224 | tf_op jit(solution)/shard_map/all_gather | solution.py:45
  7.9 236.0 %all-reduce.3.cloned.1.call-start = ((), (), s32[]{:S(2)}) async-start(), calls=%async_computation.3 | async-start | bytes 18350080 | tf_op jit(solution)/shard_map/psum | solution.py:54
  13.3 5.5 %copy-start.1 = (s32[512,64]{0,1:T(8,128)S(1)}, s32[512,64]{0,1:T(8,128)}, u32[]{:S(2)}) copy-start(s32[512,64]{0,1:T(8,128)} %param.10) | copy-start | bytes 393220
  18.8 12.0 %copy-start.2 = (bf16[896,2048]{1,0:T(8,128)(2,1)S(1)}, bf16[896,2048]{1,0:T(8,128)(2,1)}, u32[]{:S(2)}) copy-start(bf16[896,2048]{1,0:T(8,128)(2,1)} %param.13) | copy-start | bytes 11010052
  30.8 3.7 copy-start
  30.8 3.7 copy-start.3
  34.5 3.6 copy-start.6
  60.6 6.4 %copy-start.4 = (bf16[2048,896]{1,0:T(8,128)(2,1)S(1)}, bf16[2048,896]{1,0:T(8,128)(2,1)}, u32[]{:S(2)}) copy-start(bf16[2048,896]{1,0:T(8,128)(2,1)} %param.11) | copy-start | bytes 11010052
  60.6 6.4 %copy-start.8 = (bf16[512,2048]{1,0:T(8,128)(2,1)S(1)}, bf16[512,2048]{1,0:T(8,128)(2,1)}, u32[]{:S(2)}) copy-start(bf16[512,2048]{1,0:T(8,128)(2,1)} %all-gather.2.cloned.1.call-done) | copy-start | bytes 6291460
  70.6 272.5 %reduce-scatter.2.cloned.1.call-start = ((), (), s32[]{:S(2)}) async-start(), calls=%async_computation.2 | async-start | bytes 4456448 | tf_op jit(solution)/shard_map/reduce_scatter | solution.py:58
  243.9 6.4 %copy-start.7 = (bf16[2048,896]{1,0:T(8,128)(2,1)S(1)}, bf16[2048,896]{1,0:T(8,128)(2,1)}, u32[]{:S(2)}) copy-start(bf16[2048,896]{1,0:T(8,128)(2,1)} %param.12) | copy-start | bytes 11010052
  243.9 6.4 %copy-start.9 = (f32[512,896]{1,0:T(8,128)S(1)}, f32[512,896]{1,0:T(8,128)}, u32[]{:S(2)}) copy-start(f32[512,896]{1,0:T(8,128)} %get-tuple-element.3) | copy-start | bytes 5505028
  243.9 6.4 %copy-start.11 = (f32[512,896]{1,0:T(8,128)S(1)}, f32[512,896]{1,0:T(8,128)}, u32[]{:S(2)}) copy-start(f32[512,896]{1,0:T(8,128)} %get-tuple-element.6) | copy-start | bytes 5505028
  250.3 2.4 copy-start.5
  250.3 2.6 copy-start.10
  250.3 3.1 copy-start.12
  250.3 3.7 copy-start.13
Sparse Core Ops, SparseCore 0:
  10.5 50.0 all-gather.1
  70.7 173.0 all-reduce.2
  262.5 80.5 reduce-scatter.1
where the time goes:
time: 418 us
  waiting for transfers between devices  273 us (65%)
  blocking collectives  64.4 us (15%)
  matrix products  35.6 us (9%)
  other arithmetic  16.7 us (4%)
  between operations  13.9 us (3%)
  local copies, waits for them, and re-layouts  13.7 us (3%)
    psum x1, waiting for transfers between devices, local(): reduced = lax.psum((gate_pre, up_pre, gate_tan, up_tan, down_back), 'col')  173 us
    reduce_scatter x1, waiting for transfers between devices, local(): lax.psum_scatter(jnp.concatenate([grad_term, hess_term], axis=1).astype(j...  80.7 us
    psum x1, blocking collectives, local(): summed = lax.psum(partial_value, ('rep', 'row'))  64.4 us
    all_gather x1, waiting for transfers between devices, local(): block_rows = lax.all_gather(tokens, 'row', axis=0, tiled=True)  18.9 us
    dot_general x5, matrix products, transposed(): lax.dot_general(left, weight, (((1,), (1,)), ((), ())), preferred_element...  18.4 us
    unnamed x30, local copies, waits for them, and re-layouts  12.1 us
    convert_element_type x1, other arithmetic, local(): cotangent = decode(cot_codes, cot_scales).astype(jnp.bfloat16)  12 us
  transfers between devices with their start and end apart: 3, of which 3 were waited for; matrix products, arithmetic and copies ran while one was open for 8% of the time, Pallas kernels for 0%

commit v1 on v0

v1 whole, which is shorter than its diff:
```python
import functools

import jax
import jax.numpy as jnp
from jax import lax
from jax.experimental import pallas as pl
from jax.experimental.pallas import tpu as pltpu
from jax.sharding import PartitionSpec as P

MESH = pl.DeviceIdType.MESH
BF = jnp.bfloat16
F32 = jnp.float32
REPS, ROWS, COLS = 2, 16, 4
CHIPS = ROWS // 2
NCH = 4
SUB = 8
CT = ROWS * SUB
OWN = CT // COLS
HALF = OWN // 2
FE = 2048
HI = 896
HI2, HI3 = 2 * HI, 3 * HI
NT = (((1,), (1,)), ((), ()))


def aligned(value, step):
    return pl.multiple_of(value, step)


def kernel(
    tok, bits_hbm, codes_hbm, scales_hbm, wg_hbm, wu_hbm, wd_hbm,
    grad_out, hess_out, diag_out,
    w, wd, bits, codes, scales, spread, signs, cot, gathered, ordered,
    part1, part2, in1, in2, red1, red2, terms, total, mine,
    pair_out, pair_in, row_out, row_in, dsum, dbuf1, dbuf2, res,
    load_sem, tok_send, tok_recv, sib_send, sib_recv,
    rs1_send, rs1_recv, rs2_send, rs2_recv, ag1_send, ag1_recv, ag2_send, ag2_recv,
    pair_send, pair_recv, row_send, row_recv, d1_send, d1_recv, d2_send, d2_recv,
):
    rep = lax.axis_index("rep")
    row = lax.axis_index("row")
    col = lax.axis_index("col")
    core = lax.rem(row, 2)
    chip = row // 2
    sib = row + 1 - 2 * core
    left = lax.rem(col + COLS - 1, COLS)
    right = lax.rem(col + 1, COLS)
    opp = lax.rem(col + 2, COLS)
    sides = (left, right)

    def peer(step):
        other = lax.rem(chip + step, CHIPS)
        return other, 2 * other + core

    def load_bits(k):
        return pltpu.make_async_copy(bits_hbm.at[:, k], bits.at[k], load_sem.at[k])

    def load_codes(k):
        return pltpu.make_async_copy(codes_hbm.at[:, k], codes.at[k], load_sem.at[NCH + k])

    load_wg = pltpu.make_async_copy(wg_hbm, w.at[:, pl.ds(0, HI)], load_sem.at[2 * NCH])
    load_wu = pltpu.make_async_copy(wu_hbm, w.at[:, pl.ds(HI, HI)], load_sem.at[2 * NCH + 1])
    load_wd = pltpu.make_async_copy(wd_hbm, wd, load_sem.at[2 * NCH + 2])
    load_sc = pltpu.make_async_copy(scales_hbm, scales, load_sem.at[2 * NCH + 3])
    load_bits(0).start()
    load_wg.start()
    load_wu.start()
    load_codes(0).start()
    load_sc.start()
    load_wd.start()
    for k in range(1, NCH):
        load_bits(k).start()
        load_codes(k).start()

    barrier = pltpu.get_barrier_semaphore()
    for side in sides:
        pl.semaphore_signal(barrier, inc=1, device_id={"col": side}, device_id_type=MESH)
    pl.semaphore_signal(barrier, inc=1, device_id={"row": sib}, device_id_type=MESH)
    for other_row in (row, sib):
        pl.semaphore_signal(
            barrier, inc=1, device_id={"rep": 1 - rep, "row": other_row}, device_id_type=MESH
        )
    for step in range(1, CHIPS):
        pl.semaphore_signal(barrier, inc=1, device_id={"row": peer(step)[1]}, device_id_type=MESH)
    pl.semaphore_wait(barrier, 5 + CHIPS - 1)

    def remote(src, dst, send, recv, where):
        return pltpu.make_async_remote_copy(
            src_ref=src, dst_ref=dst, send_sem=send, recv_sem=recv, device_id=where, device_id_type=MESH
        )

    def send_tok(step):
        other, where = peer(step)
        return remote(tok, gathered.at[row], tok_send.at[other], tok_recv.at[chip], {"row": where})

    def recv_tok(other):
        block = gathered.at[2 * other + core]
        return remote(block, block, tok_send.at[other], tok_recv.at[other], {"row": sib})

    def own_to_sib():
        return remote(tok, gathered.at[row], sib_send.at[chip], sib_recv.at[chip], {"row": sib})

    def relay(other):
        block = gathered.at[2 * other + core]
        return remote(block, block, sib_send.at[other], sib_recv.at[other], {"row": sib})

    own_to_sib().start()
    for step in range(1, CHIPS):
        send_tok(step).start()
    gathered[row] = tok[...]

    lanes = lax.broadcasted_iota(jnp.int32, spread.shape, 1) // 32
    spread[...] = (lanes == lax.broadcasted_iota(jnp.int32, spread.shape, 0)).astype(F32).astype(BF)

    def rs1(batch, k, side):
        part, inn = ((part1, in1), (part2, in2))[batch]
        src = part.at[k, pl.ds(aligned(OWN * opp + HALF * side, HALF), HALF)]
        at = NCH * batch + k
        return remote(
            src, inn.at[side, k], rs1_send.at[side, at], rs1_recv.at[side, at], {"col": sides[side]}
        )

    def rs2(batch, k, side):
        part, red = ((part1, red1), (part2, red2))[batch]
        src = part.at[k, pl.ds(aligned(OWN * sides[side], OWN), OWN)]
        at = NCH * batch + k
        return remote(
            src, red.at[side, k], rs2_send.at[side, at], rs2_recv.at[side, at], {"col": sides[side]}
        )

    def fold(batch, k):
        part, inn = ((part1, in1), (part2, in2))[batch]
        for side in range(2):
            rs1(batch, k, side).wait_recv()
            rows = pl.ds(aligned(OWN * sides[side] + HALF * side, HALF), HALF)
            part[k, rows] = (part[k, rows].astype(F32) + inn[side, k].astype(F32)).astype(BF)
            rs2(batch, k, side).start()

    def forward1(k):
        load_bits(k).wait()
        signs[k] = (2 * bits[k].reshape(CT, FE) - 1).astype(F32).astype(BF)

        @pl.when(k == 0)
        def _():
            load_wg.wait()
            load_wu.wait()

        @pl.loop(0, HI2 // 256)
        def _(n):
            cols = pl.ds(aligned(n * 256, 256), 256)
            part1[k, :, cols] = jnp.dot(signs[k], w[:, cols], preferred_element_type=F32).astype(BF)

        load_codes(k).wait()

        @pl.when(k == 0)
        def _():
            load_sc.wait()
            load_wd.wait()

        power = (lax.shift_left(1, scales[:, k].reshape(CT, FE // 32) + 2).astype(F32) * 2.0**-7).astype(BF)

        @pl.loop(0, FE // 512)
        def _(n):
            cols = pl.ds(aligned(n * 512, 512), 512)
            code = codes[k, :, :, cols].reshape(CT, 512)
            size = lax.shift_left((code & 7) | 8, ((code >> 3) & 15) - 5)
            value = jnp.where(code >= 128, -size, size).astype(F32)
            wide = jnp.dot(power, spread[:, cols], preferred_element_type=F32)
            cot[:, cols] = (value * wide).astype(BF)

        for start in range(0, HI, 256):
            wide = min(256, HI - start)
            part1[k, :, pl.ds(HI2 + start, wide)] = lax.dot_general(
                cot[...], wd[pl.ds(start, wide), :], NT, preferred_element_type=F32
            ).astype(BF)
        for side in range(2):
            rs1(0, k, side).start()

    def forward2(k):
        @pl.loop(0, HI2 // 256)
        def _(n):
            cols = pl.ds(aligned(n * 256, 256), 256)
            part2[k, :, cols] = jnp.dot(ordered[k], w[:, cols], preferred_element_type=F32).astype(BF)

        for side in range(2):
            rs1(1, k, side).start()

    def gather_tokens():
        @pl.loop(1, CHIPS)
        def _(step):
            other = peer(step)[0]
            recv_tok(other).wait_recv()
            relay(other).start()

        @pl.loop(0, CHIPS)
        def _(other):
            relay(other).wait_recv()

        @pl.loop(0, CHIPS)
        def _(q):
            for h in range(NCH // 2):
                rows = pl.ds(2 * SUB * h, 2 * SUB)
                even = gathered[2 * q, rows].astype(F32)
                odd = gathered[2 * q + 1, rows].astype(F32)
                out = pl.ds(aligned(2 * SUB * q, 2 * SUB), 2 * SUB)
                ordered[2 * h, out] = jnp.concatenate([even[:SUB], odd[:SUB]], axis=0).astype(BF)
                ordered[2 * h + 1, out] = jnp.concatenate([even[SUB:], odd[SUB:]], axis=0).astype(BF)

    @pl.loop(0, 2 * NCH + 1)
    def _(s):
        @pl.when(s < NCH)
        def _():
            forward1(s)

        @pl.when(s == NCH)
        def _():
            gather_tokens()

        @pl.when(jnp.logical_and(s >= NCH, s < 2 * NCH))
        def _():
            forward2(s - NCH)

        @pl.when(jnp.logical_and(s >= 1, s <= NCH))
        def _():
            fold(0, s - 1)

        @pl.when(s > NCH)
        def _():
            fold(1, s - 1 - NCH)

    def ag1(k, side):
        block = terms.at[k, :, pl.ds(aligned(OWN * col, OWN), OWN)]
        return remote(block, block, ag1_send.at[side, k], ag1_recv.at[side, k], {"col": sides[side]})

    def ag2(k, side):
        rows = pl.ds(aligned(OWN * sides[1 - side] + HALF * side, HALF), HALF)
        block = terms.at[k, :, rows]
        return remote(block, block, ag2_send.at[side, k], ag2_recv.at[side, k], {"col": sides[side]})

    def work_terms(k):
        for batch in range(2):
            for side in range(2):
                rs2(batch, k, side).wait_recv()
        rows = pl.ds(aligned(OWN * col, OWN), OWN)

        def full(part, red, start):
            cols = pl.ds(start, 128)
            return part[k, rows, cols].astype(F32) + red[0, k, :, cols].astype(F32) + red[1, k, :, cols].astype(F32)

        for start in range(0, HI, 128):
            gate_tan = full(part1, red1, start)
            up_tan = full(part1, red1, HI + start)
            down_back = full(part1, red1, HI2 + start)
            gate_pre = full(part2, red2, start)
            up_pre = full(part2, red2, HI + start)
            sig = 1.0 / (1.0 + jnp.exp(-gate_pre))
            rest = 1.0 - sig
            first = sig * (1.0 + gate_pre * rest)
            second = sig * rest * (2.0 + gate_pre * (1.0 - 2.0 * sig))
            down_first = down_back * first
            terms[k, 0, rows, pl.ds(start, 128)] = (down_first * up_pre).astype(BF)
            terms[k, 0, rows, pl.ds(HI + start, 128)] = (down_back * gate_pre * sig).astype(BF)
            terms[k, 1, rows, pl.ds(start, 128)] = (
                down_back * (up_tan * first + up_pre * second * gate_tan)
            ).astype(BF)
            terms[k, 1, rows, pl.ds(HI + start, 128)] = (down_first * gate_tan).astype(BF)
        for side in range(2):
            ag1(k, side).start()

    def forward_terms(k):
        for side in range(2):
            ag1(k, side).wait_recv()
            ag2(k, side).start()

    def pair(k):
        return remote(pair_out.at[k], pair_in.at[k], pair_send.at[k], pair_recv.at[k], {"row": sib})

    def row_copy(k, step):
        other, where = peer(step)
        return remote(
            row_out.at[k, other], row_in.at[k, chip], row_send.at[k, other], row_recv.at[k, chip], {"row": where}
        )

    def row_wait(k, other):
        return remote(
            row_out.at[k, other], row_in.at[k, other], row_send.at[k, other], row_recv.at[k, other], {"row": sib}
        )

    dsum[...] = jnp.zeros_like(dsum)

    def backward(k):
        for side in range(2):
            ag2(k, side).wait_recv()

        @pl.loop(0, FE // 512)
        def _(n):
            cols = pl.ds(aligned(n * 512, 512), 512)
            out = lax.dot_general(
                terms[k].reshape(2 * CT, HI2), w[cols, :], NT, preferred_element_type=F32
            )
            res[:, cols] = out
            prod = out[CT:] * signs[k, :, cols].astype(F32)
            dsum[:, cols] += jnp.sum(prod.reshape(CT // 8, 8, 512), axis=0)

        slot = lax.rem(k, 2)

        @pl.loop(0, CHIPS)
        def _(m):
            rows = pl.ds(aligned(2 * SUB * m, 2 * SUB), 2 * SUB)
            for keep, at in ((False, 1 - core), (True, core)):
                first = aligned(2 * SUB * m + SUB * at, SUB)
                both = jnp.concatenate(
                    [res[pl.ds(first, SUB), :], res[pl.ds(aligned(CT + first, SUB), SUB), :]], axis=0
                )
                if keep:
                    mine[slot, rows] = both
                else:
                    pair_out[k, rows] = both.astype(BF)

        pair(k).start()

    def send_rows(k):
        pair(k).wait_recv()
        slot = lax.rem(k, 2)

        @pl.loop(0, CHIPS)
        def _(m):
            rows = pl.ds(aligned(2 * SUB * m, 2 * SUB), 2 * SUB)
            row_out[k, m] = (mine[slot, rows] + pair_in[k, rows].astype(F32)).astype(BF)

        @pl.loop(1, CHIPS)
        def _(step):
            row_copy(k, step).start()

        row_in[k, chip] = row_out[k, chip]

    def finish(k):
        @pl.loop(1, CHIPS)
        def _(step):
            row_wait(k, peer(step)[0]).wait_recv()

        total_k = row_in[k, 0].astype(F32)
        for m in range(1, CHIPS):
            total_k = total_k + row_in[k, m].astype(F32)
        total[0, pl.ds(aligned(SUB * k, SUB), SUB)] = total_k[:SUB]
        total[1, pl.ds(aligned(SUB * k, SUB), SUB)] = total_k[SUB:]

    def d1(step):
        other, where = peer(step)
        return remote(dbuf1.at[chip], dbuf1.at[chip], d1_send.at[other], d1_recv.at[chip], {"row": where})

    def d1_wait(other):
        return remote(dbuf1.at[other], dbuf1.at[other], d1_send.at[other], d1_recv.at[other], {"row": sib})

    quad = 2 * rep + core

    def d2(which):
        where = ({"row": sib}, {"rep": 1 - rep}, {"rep": 1 - rep, "row": sib})[which]
        return remote(dbuf2.at[quad], dbuf2.at[quad], d2_send.at[which], d2_recv.at[which], where)

    @pl.loop(0, NCH + 4)
    def _(s):
        @pl.when(s < NCH)
        def _():
            work_terms(s)

        @pl.when(jnp.logical_and(s >= 1, s < NCH + 1))
        def _():
            forward_terms(s - 1)

        @pl.when(jnp.logical_and(s >= 3, s < NCH + 3))
        def _():
            send_rows(s - 3)

        @pl.when(jnp.logical_and(s >= 2, s < NCH + 2))
        def _():
            backward(s - 2)

        @pl.when(s == NCH + 1)
        def _():
            dbuf1[chip] = jnp.sum(dsum[...], axis=0, keepdims=True)
            for step in range(1, CHIPS):
                d1(step).start()

        @pl.when(s == NCH + 2)
        def _():
            for step in range(1, CHIPS):
                d1_wait(peer(step)[0]).wait_recv()
            dbuf2[quad] = jnp.sum(dbuf1[...], axis=0)
            for which in range(3):
                d2(which).start()

        @pl.when(s >= 4)
        def _():
            finish(s - 4)

    grad_out[...] = total[0].astype(BF)
    hess_out[...] = total[1].astype(BF)
    for which in range(3):
        d2(which).wait_recv()
    diag_out[...] = jnp.sum(dbuf2[...], axis=0) * (1.0 / (REPS * ROWS * NCH * SUB))

    own_to_sib().wait_send()
    for which in range(3):
        d2(which).wait_send()

    @pl.loop(1, CHIPS)
    def _(step):
        send_tok(step).wait_send()
        relay(peer(step)[0]).wait_send()
        d1(step).wait_send()

    @pl.loop(0, NCH)
    def _(k):
        for side in range(2):
            for batch in range(2):
                rs1(batch, k, side).wait_send()
                rs2(batch, k, side).wait_send()
            ag1(k, side).wait_send()
            ag2(k, side).wait_send()
        pair(k).wait_send()

        @pl.loop(1, CHIPS)
        def _(step):
            row_copy(k, step).wait_send()


def local(tokens, probe_bits, cot_codes, cot_scales, w_gate, w_up, w_down):
    split = (ROWS, NCH, SUB)
    vm = pl.BlockSpec(memory_space=pltpu.VMEM)
    hbm = pl.BlockSpec(memory_space=pl.ANY)
    dma = pltpu.SemaphoreType.DMA
    grad, hess, diag = pl.pallas_call(
        kernel,
        out_shape=(
            jax.ShapeDtypeStruct((NCH * SUB, FE), BF),
            jax.ShapeDtypeStruct((NCH * SUB, FE), BF),
            jax.ShapeDtypeStruct((1, FE), F32),
        ),
        in_specs=[vm] + [hbm] * 6,
        out_specs=[vm] * 3,
        scratch_shapes=[
            pltpu.VMEM((FE, HI2), BF),
            pltpu.VMEM((HI, FE), BF),
            pltpu.VMEM((NCH, ROWS, SUB, FE), jnp.int32),
            pltpu.VMEM((NCH, ROWS, SUB, FE), jnp.int32),
            pltpu.VMEM((ROWS, NCH, SUB, FE // 32), jnp.int32),
            pltpu.VMEM((FE // 32, FE), BF),
            pltpu.VMEM((NCH, CT, FE), BF),
            pltpu.VMEM((CT, FE), BF),
            pltpu.VMEM((ROWS, NCH * SUB, FE), BF),
            pltpu.VMEM((NCH, CT, FE), BF),
            pltpu.VMEM((NCH, CT, HI3), BF),
            pltpu.VMEM((NCH, CT, HI2), BF),
            pltpu.VMEM((2, NCH, HALF, HI3), BF),
            pltpu.VMEM((2, NCH, HALF, HI2), BF),
            pltpu.VMEM((2, NCH, OWN, HI3), BF),
            pltpu.VMEM((2, NCH, OWN, HI2), BF),
            pltpu.VMEM((NCH, 2, CT, HI2), BF),
            pltpu.VMEM((2, NCH * SUB, FE), F32),
            pltpu.VMEM((2, CT, FE), F32),
            pltpu.VMEM((NCH, CT, FE), BF),
            pltpu.VMEM((NCH, CT, FE), BF),
            pltpu.VMEM((NCH, CHIPS, 2 * SUB, FE), BF),
            pltpu.VMEM((NCH, CHIPS, 2 * SUB, FE), BF),
            pltpu.VMEM((8, FE), F32),
            pltpu.VMEM((CHIPS, 1, FE), F32),
            pltpu.VMEM((4, 1, FE), F32),
            pltpu.VMEM((2 * CT, FE), F32),
            dma((2 * NCH + 4,)),
            dma((CHIPS,)), dma((CHIPS,)), dma((CHIPS,)), dma((CHIPS,)),
            dma((2, 2 * NCH)), dma((2, 2 * NCH)), dma((2, 2 * NCH)), dma((2, 2 * NCH)),
            dma((2, NCH)), dma((2, NCH)), dma((2, NCH)), dma((2, NCH)),
            dma((NCH,)), dma((NCH,)),
            dma((NCH, CHIPS)), dma((NCH, CHIPS)),
            dma((CHIPS,)), dma((CHIPS,)), dma((3,)), dma((3,)),
        ],
        compiler_params=pltpu.CompilerParams(
            collective_id=0, has_side_effects=True, vmem_limit_bytes=63 * 2**20
        ),
    )(
        tokens,
        probe_bits.reshape(split + (FE,)),
        cot_codes.reshape(split + (FE,)),
        cot_scales.reshape(split + (FE // 32,)),
        w_gate,
        w_up,
        w_down,
    )
    return grad, hess, diag.reshape(FE)


def solution(mesh):
    in_specs = (
        P(("rep", "row"), "col"),
        P("rep", "col"),
        P("rep", "col"),
        P("rep", "col"),
        P("col", "row"),
        P("col", "row"),
        P("row", "col"),
    )
    out_specs = (P(("rep", "row"), "col"), P(("rep", "row"), "col"), P("col"))
    return jax.shard_map(local, mesh=mesh, in_specs=in_specs, out_specs=out_specs, check_vma=False)
```

time: 418 us -> 112 us (0.27)
  waiting for transfers between devices: 273 us -> 0 us
  Pallas kernels: 0 us -> 105 us
  blocking collectives: 64.4 us -> 0 us
  matrix products: 35.6 us -> 0 us
  other arithmetic: 16.7 us -> 0 us
  between operations: 13.9 us -> 0.64 us
  local copies, waits for them, and re-layouts: 13.7 us -> 6.16 us
    psum x1 -> x0, waiting for transfers between devices: 173 us -> none  [local(): reduced = lax.psum((gate_pre, up_pre, gate_tan, up_tan, down_back), 'col')]
    pallas_call x0 -> x1, Pallas kernels: none -> 105 us  [local(): pl.pallas_call(kernel, out_shape=(jax.ShapeDtypeStruct((NCH * SUB, FE), B...]
    reduce_scatter x1 -> x0, waiting for transfers between devices: 80.7 us -> none  [local(): lax.psum_scatter(jnp.concatenate([grad_term, hess_term], axis=1).astype(j...]
    psum x1 -> x0, blocking collectives: 64.4 us -> none  [local(): summed = lax.psum(partial_value, ('rep', 'row'))]
    dot_general x9 -> x0, matrix products: 35.6 us -> none  [the longest x5 18.4 us: transposed(): lax.dot_general(left, weight, (((1,), (1,)), ((), ())), preferred_element...]
    all_gather x1 -> x0, waiting for transfers between devices: 18.9 us -> none  [local(): block_rows = lax.all_gather(tokens, 'row', axis=0, tiled=True)]
    convert_element_type x1 -> x0, other arithmetic: 12 us -> none  [local(): cotangent = decode(cot_codes, cot_scales).astype(jnp.bfloat16)]
    unnamed x30 -> x4, local copies, waits for them, and re-layouts: 12.1 us -> 6.16 us
  transfers between devices with their start and end apart: 3 -> 0, of which waited for: 3 -> 0; matrix products, arithmetic and copies ran while one was open for 8% -> 0% of each run, Pallas kernels for 0% -> 0%
where the time goes in v1:
time: 112 us; the launch traced here: 111 us
  Pallas kernels  105 us (94%)
  local copies, waits for them, and re-layouts  6.16 us (6%)
    pallas_call x1, Pallas kernels, local(): pl.pallas_call(kernel, out_shape=(jax.ShapeDtypeStruct((NCH * SUB, FE), B...  105 us
    unnamed x4, local copies, waits for them, and re-layouts  6.16 us

profile of v1, /device:TPU:0, one launch (start us, length us, event | category | flops | bytes accessed | tf_op | source)
XLA Modules:
  0.0 111.5 jit_solution(9134504405133731583)
XLA Ops:
  0.6 1.7 %copy.10 = s32[512,64]{1,0:T(8,128)} copy(s32[512,64]{0,1:T(8,128)} %param.10) | data formatting | bytes 262144 | tf_op args[3]
  2.4 104.7 %shard_map.94 = (bf16[32,2048]{1,0:T(8,128)(2,1)}, bf16[32,2048]{1,0:T(8,128)(2,1)}, f32[1,2048]{1,0:T(1,128)}) custom-call(bf16[32,2048]{1,0:T(8,128)(2,1)} %tok.1, s32[16,4,8,2048]{3,2,1,0:T(8,128)} %bitcast.4, s32[16,4,8,2048]{3,2,1,0:T(8,128)} %bitcast.5, s32[16,4,8,64]{3,2,1,0:T(8,128)} %bitcast.6, bf16[2048,896]{1,0:T(8,128)(2,1)} %wg_hbm.1, ...), custom_call_target="tpu_custom_call" | custom-call | tf_op jit(solution)/shard_map/pallas_call | solution.py:433
  107.1 1.6 %copy.14 = bf16[32,2048]{1,0:T(8,128)(2,1)} copy(bf16[32,2048]{1,0:T(8,128)(2,1)} %get-tuple-element.12) | data formatting | bytes 262144
  108.6 1.6 %copy.15 = bf16[32,2048]{1,0:T(8,128)(2,1)} copy(bf16[32,2048]{1,0:T(8,128)(2,1)} %get-tuple-element.13) | data formatting | bytes 262144
  110.2 1.3 %copy.16 = f32[2048]{0:T(1024)} copy(f32[2048]{0:T(1024)} %bitcast.7) | data formatting | bytes 16384

commit v2 on v1

v2 whole, which is shorter than its diff:
```python
import functools

import jax
import jax.numpy as jnp
from jax import lax
from jax.experimental import pallas as pl
from jax.experimental.pallas import tpu as pltpu
from jax.sharding import PartitionSpec as P

MESH = pl.DeviceIdType.MESH
BF = jnp.bfloat16
F32 = jnp.float32
REPS, ROWS, COLS = 2, 16, 4
CHIPS = ROWS // 2
NCH = 4
SUB = 8
CT = ROWS * SUB
OWN = CT // COLS
HALF = OWN // 2
FE = 2048
HI = 896
HI2 = 2 * HI
FH = FE // 2
NT = (((1,), (1,)), ((), ()))


def aligned(value, step):
    return pl.multiple_of(value, step)


def kernel(
    tok, bits_hbm, codes_hbm, scales_hbm, wg_hbm, wu_hbm, wd_hbm,
    total, diag_out,
    w, wd, bits, codes, scales, spread, power, signs, cot, gathered, ordered,
    part0, part1, part2, in0, in1, in2, red0, red1, red2, terms, mine,
    pair_out, pair_in, row_out, row_in, dsum, dbuf1, dbuf2, res,
    load_sem, tok_send, tok_recv, sib_send, sib_recv,
    rs1_send, rs1_recv, rs2_send, rs2_recv, ag1_send, ag1_recv, ag2_send, ag2_recv,
    pair_send, pair_recv, row_send, row_recv, d1_send, d1_recv, d2_send, d2_recv,
):
    rep = lax.axis_index("rep")
    row = lax.axis_index("row")
    col = lax.axis_index("col")
    core = lax.rem(row, 2)
    chip = row // 2
    sib = row + 1 - 2 * core
    left = lax.rem(col + COLS - 1, COLS)
    right = lax.rem(col + 1, COLS)
    opp = lax.rem(col + 2, COLS)
    sides = (left, right)

    def peer(step):
        other = lax.rem(chip + step, CHIPS)
        return other, 2 * other + core

    def load_bits(k):
        return pltpu.make_async_copy(bits_hbm.at[:, k], bits.at[k], load_sem.at[k])

    def load_codes(k):
        return pltpu.make_async_copy(codes_hbm.at[:, k], codes.at[k], load_sem.at[NCH + k])

    load_wg = pltpu.make_async_copy(wg_hbm, w.at[:, pl.ds(0, HI)], load_sem.at[2 * NCH])
    load_wu = pltpu.make_async_copy(wu_hbm, w.at[:, pl.ds(HI, HI)], load_sem.at[2 * NCH + 1])
    load_wd = pltpu.make_async_copy(wd_hbm, wd, load_sem.at[2 * NCH + 2])
    load_sc = pltpu.make_async_copy(scales_hbm, scales, load_sem.at[2 * NCH + 3])
    load_sc.start()
    load_codes(0).start()
    load_codes(1).start()
    load_wd.start()
    load_codes(2).start()
    load_codes(3).start()
    load_bits(0).start()
    load_wg.start()
    load_wu.start()
    for k in range(1, NCH):
        load_bits(k).start()

    barrier = pltpu.get_barrier_semaphore()
    for side in sides:
        pl.semaphore_signal(barrier, inc=1, device_id={"col": side}, device_id_type=MESH)
    pl.semaphore_signal(barrier, inc=1, device_id={"row": sib}, device_id_type=MESH)
    for other_row in (row, sib):
        pl.semaphore_signal(
            barrier, inc=1, device_id={"rep": 1 - rep, "row": other_row}, device_id_type=MESH
        )
    for step in range(1, CHIPS):
        pl.semaphore_signal(barrier, inc=1, device_id={"row": peer(step)[1]}, device_id_type=MESH)
    pl.semaphore_wait(barrier, 5 + CHIPS - 1)

    def remote(src, dst, send, recv, where):
        return pltpu.make_async_remote_copy(
            src_ref=src, dst_ref=dst, send_sem=send, recv_sem=recv, device_id=where, device_id_type=MESH
        )

    def send_tok(step):
        other, where = peer(step)
        return remote(tok, gathered.at[row], tok_send.at[other], tok_recv.at[chip], {"row": where})

    def recv_tok(other):
        block = gathered.at[2 * other + core]
        return remote(block, block, tok_send.at[other], tok_recv.at[other], {"row": sib})

    def own_to_sib():
        return remote(tok, gathered.at[row], sib_send.at[chip], sib_recv.at[chip], {"row": sib})

    def relay(other):
        block = gathered.at[2 * other + core]
        return remote(block, block, sib_send.at[other], sib_recv.at[other], {"row": sib})

    own_to_sib().start()
    for step in range(1, CHIPS):
        send_tok(step).start()
    gathered[row] = tok[...]

    lanes = lax.broadcasted_iota(jnp.int32, spread.shape, 1) // 32
    spread[...] = (lanes == lax.broadcasted_iota(jnp.int32, spread.shape, 0)).astype(F32).astype(BF)
    at = lax.broadcasted_iota(jnp.int32, (NCH * CT, NCH * CT), 0)
    token = (at % CT) // SUB * (NCH * SUB) + at // CT * SUB + at % SUB
    pick = (token == lax.broadcasted_iota(jnp.int32, (NCH * CT, NCH * CT), 1)).astype(F32).astype(BF)
    load_sc.wait()
    raised = (lax.shift_left(1, scales[...] + 2).astype(F32) * 2.0**-7).astype(BF)
    power[...] = lax.dot_general(pick, raised, NT, preferred_element_type=F32).astype(BF)

    batches = ((part0, in0, red0, 2, 0), (part1, in1, red1, 1, 2), (part2, in2, red2, 1, 2 + NCH))

    def rs1(batch, k, side):
        part, inn, _, n, base = batches[batch]
        ks = pl.ds(k * n, n)
        src = part.at[ks, pl.ds(aligned(OWN * opp + HALF * side, HALF), HALF)]
        return remote(
            src, inn.at[side, ks], rs1_send.at[side, base + k], rs1_recv.at[side, base + k], {"col": sides[side]}
        )

    def rs2(batch, k, side):
        part, _, red, n, base = batches[batch]
        ks = pl.ds(k * n, n)
        src = part.at[ks, pl.ds(aligned(OWN * sides[side], OWN), OWN)]
        return remote(
            src, red.at[side, ks], rs2_send.at[side, base + k], rs2_recv.at[side, base + k], {"col": sides[side]}
        )

    def start_rs1(batch, k):
        for side in range(2):
            rs1(batch, k, side).start()

    def fold(batch, k):
        part, inn, _, n, _ = batches[batch]
        for side in range(2):
            rs1(batch, k, side).wait_recv()
            rows = pl.ds(aligned(OWN * sides[side] + HALF * side, HALF), HALF)
            for i in range(n):
                at = k * n + i
                part[at, rows] = (part[at, rows].astype(F32) + inn[side, at].astype(F32)).astype(BF)
            rs2(batch, k, side).start()

    def down(p):
        for i in range(2):
            load_codes(2 * p + i).wait()

        @pl.loop(0, FE // 512)
        def _(n):
            cols = pl.ds(aligned(n * 512, 512), 512)
            code = codes[pl.ds(2 * p, 2), :, :, cols].reshape(2 * CT, 512)
            size = lax.shift_left((code & 7) | 8, ((code >> 3) & 15) - 5)
            value = jnp.where(code >= 128, -size, size).astype(F32)
            wide = jnp.dot(
                power[pl.ds(aligned(2 * CT * p, 2 * CT), 2 * CT), :], spread[:, cols], preferred_element_type=F32
            )
            cot[:, cols] = (value * wide).astype(BF)

        @pl.when(p == 0)
        def _():
            load_wd.wait()

        part0[pl.ds(2 * p, 2)] = (
            lax.dot_general(cot[...], wd[...], NT, preferred_element_type=F32).astype(BF).reshape(2, CT, HI)
        )
        start_rs1(0, p)

    def tangent(k):
        load_bits(k).wait()
        signs[k] = (2 * bits[k].reshape(CT, FE) - 1).astype(F32).astype(BF)

        @pl.when(k == 0)
        def _():
            load_wg.wait()
            load_wu.wait()

        part1[k] = jnp.dot(signs[k], w[...], preferred_element_type=F32).astype(BF)
        start_rs1(1, k)

    def primal(k):
        part2[k] = jnp.dot(ordered[k], w[...], preferred_element_type=F32).astype(BF)
        start_rs1(2, k)

    def gather_tokens():
        @pl.loop(1, CHIPS)
        def _(step):
            other = peer(step)[0]
            recv_tok(other).wait_recv()
            relay(other).start()

    def order_tokens():
        @pl.loop(0, CHIPS)
        def _(other):
            relay(other).wait_recv()

        @pl.loop(0, CHIPS)
        def _(q):
            for h in range(NCH // 2):
                rows = pl.ds(2 * SUB * h, 2 * SUB)
                even = gathered[2 * q, rows].astype(F32)
                odd = gathered[2 * q + 1, rows].astype(F32)
                out = pl.ds(aligned(2 * SUB * q, 2 * SUB), 2 * SUB)
                ordered[2 * h, out] = jnp.concatenate([even[:SUB], odd[:SUB]], axis=0).astype(BF)
                ordered[2 * h + 1, out] = jnp.concatenate([even[SUB:], odd[SUB:]], axis=0).astype(BF)

    @pl.loop(0, 2)
    def _(p):
        down(p)

    @pl.loop(0, NCH)
    def _(s):
        @pl.when(s < 2)
        def _():
            fold(0, s)

        tangent(s)

        @pl.when(s >= 2)
        def _():
            fold(1, s - 2)

    gather_tokens()
    order_tokens()

    @pl.loop(0, NCH)
    def _(s):
        primal(s)

        @pl.when(s < 2)
        def _():
            fold(1, s + 2)

        @pl.when(s >= 2)
        def _():
            fold(2, s - 2)

    fold(2, 2)

    def ag1(k, side):
        block = terms.at[k, :, pl.ds(aligned(OWN * col, OWN), OWN)]
        return remote(block, block, ag1_send.at[side, k], ag1_recv.at[side, k], {"col": sides[side]})

    def ag2(k, side):
        rows = pl.ds(aligned(OWN * sides[1 - side] + HALF * side, HALF), HALF)
        block = terms.at[k, :, rows]
        return remote(block, block, ag2_send.at[side, k], ag2_recv.at[side, k], {"col": sides[side]})

    def work_terms(k):
        for side in range(2):
            rs2(1, k, side).wait_recv()
            rs2(2, k, side).wait_recv()

        @pl.when(lax.rem(k, 2) == 0)
        def _():
            for side in range(2):
                rs2(0, k // 2, side).wait_recv()

        rows = pl.ds(aligned(OWN * col, OWN), OWN)

        def full(part, red, start):
            cols = pl.ds(start, 128)
            return part[k, rows, cols].astype(F32) + red[0, k, :, cols].astype(F32) + red[1, k, :, cols].astype(F32)

        for start in range(0, HI, 128):
            gate_tan = full(part1, red1, start)
            up_tan = full(part1, red1, HI + start)
            down_back = full(part0, red0, start)
            gate_pre = full(part2, red2, start)
            up_pre = full(part2, red2, HI + start)
            sig = 1.0 / (1.0 + jnp.exp(-gate_pre))
            rest = 1.0 - sig
            first = sig * (1.0 + gate_pre * rest)
            second = sig * rest * (2.0 + gate_pre * (1.0 - 2.0 * sig))
            down_first = down_back * first
            terms[k, 0, rows, pl.ds(start, 128)] = (down_first * up_pre).astype(BF)
            terms[k, 0, rows, pl.ds(HI + start, 128)] = (down_back * gate_pre * sig).astype(BF)
            terms[k, 1, rows, pl.ds(start, 128)] = (
                down_back * (up_tan * first + up_pre * second * gate_tan)
            ).astype(BF)
            terms[k, 1, rows, pl.ds(HI + start, 128)] = (down_first * gate_tan).astype(BF)
        for side in range(2):
            ag1(k, side).start()

    def forward_terms(k):
        for side in range(2):
            ag1(k, side).wait_recv()
            ag2(k, side).start()

    def pair(k, h):
        return remote(
            pair_out.at[k, h], pair_in.at[k, h], pair_send.at[k, h], pair_recv.at[k, h], {"row": sib}
        )

    def row_copy(k, h, step):
        other, where = peer(step)
        return remote(
            row_out.at[k, h, other], row_in.at[k, h, chip],
            row_send.at[k, h, other], row_recv.at[k, h, chip], {"row": where},
        )

    def row_wait(k, h, other):
        return remote(
            row_out.at[k, h, other], row_in.at[k, h, other],
            row_send.at[k, h, other], row_recv.at[k, h, other], {"row": sib},
        )

    dsum[...] = jnp.zeros_like(dsum)

    def backward(k):
        for side in range(2):
            ag2(k, side).wait_recv()
        slot = lax.rem(k, 2)

        @pl.loop(0, 2)
        def _(h):
            cols = pl.ds(aligned(h * FH, FH), FH)
            res[...] = lax.dot_general(
                terms[k].reshape(2 * CT, HI2), w[cols, :], NT, preferred_element_type=F32
            )
            prod = res[CT:, :] * signs[k, :, cols].astype(F32)
            dsum[:, cols] += jnp.sum(prod.reshape(CT // 8, 8, FH), axis=0)

            @pl.loop(0, CHIPS)
            def _(m):
                rows = pl.ds(aligned(2 * SUB * m, 2 * SUB), 2 * SUB)
                for keep, at in ((False, 1 - core), (True, core)):
                    first = aligned(2 * SUB * m + SUB * at, SUB)
                    both = jnp.concatenate(
                        [res[pl.ds(first, SUB), :], res[pl.ds(aligned(CT + first, SUB), SUB), :]], axis=0
                    )
                    if keep:
                        mine[slot, h, rows] = both
                    else:
                        pair_out[k, h, rows] = both.astype(BF)

            pair(k, h).start()

    def send_rows(k):
        slot = lax.rem(k, 2)

        @pl.loop(0, 2)
        def _(h):
            pair(k, h).wait_recv()

            @pl.loop(0, CHIPS)
            def _(m):
                rows = pl.ds(aligned(2 * SUB * m, 2 * SUB), 2 * SUB)
                row_out[k, h, m] = (mine[slot, h, rows] + pair_in[k, h, rows].astype(F32)).astype(BF)

            @pl.loop(1, CHIPS)
            def _(step):
                row_copy(k, h, step).start()

            row_in[k, h, chip] = row_out[k, h, chip]

    def finish(k):
        rows = pl.ds(aligned(SUB * k, SUB), SUB)
        for h in range(2):

            @pl.loop(1, CHIPS)
            def _(step):
                row_wait(k, h, peer(step)[0]).wait_recv()

            total_k = row_in[k, h, 0].astype(F32)
            for m in range(1, CHIPS):
                total_k = total_k + row_in[k, h, m].astype(F32)
            cols = pl.ds(h * FH, FH)
            total[0, rows, cols] = total_k[:SUB]
            total[1, rows, cols] = total_k[SUB:]

    def d1(step):
        other, where = peer(step)
        return remote(dbuf1.at[chip], dbuf1.at[chip], d1_send.at[other], d1_recv.at[chip], {"row": where})

    def d1_wait(other):
        return remote(dbuf1.at[other], dbuf1.at[other], d1_send.at[other], d1_recv.at[other], {"row": sib})

    quad = 2 * rep + core

    def d2(which):
        where = ({"row": sib}, {"rep": 1 - rep}, {"rep": 1 - rep, "row": sib})[which]
        return remote(dbuf2.at[quad], dbuf2.at[quad], d2_send.at[which], d2_recv.at[which], where)

    @pl.loop(0, NCH + 4)
    def _(s):
        @pl.when(s < NCH)
        def _():
            work_terms(s)

        @pl.when(s == 0)
        def _():
            fold(2, NCH - 1)

        @pl.when(jnp.logical_and(s >= 1, s < NCH + 1))
        def _():
            forward_terms(s - 1)

        @pl.when(jnp.logical_and(s >= 3, s < NCH + 3))
        def _():
            send_rows(s - 3)

        @pl.when(jnp.logical_and(s >= 2, s < NCH + 2))
        def _():
            backward(s - 2)

        @pl.when(s == NCH + 1)
        def _():
            dbuf1[chip] = jnp.sum(dsum[...], axis=0, keepdims=True)
            for step in range(1, CHIPS):
                d1(step).start()

        @pl.when(s == NCH + 2)
        def _():
            for step in range(1, CHIPS):
                d1_wait(peer(step)[0]).wait_recv()
            dbuf2[quad] = jnp.sum(dbuf1[...], axis=0)
            for which in range(3):
                d2(which).start()

        @pl.when(s >= 4)
        def _():
            finish(s - 4)

    for which in range(3):
        d2(which).wait_recv()
    diag_out[...] = jnp.sum(dbuf2[...], axis=0) * (1.0 / (REPS * ROWS * NCH * SUB))

    own_to_sib().wait_send()
    for which in range(3):
        d2(which).wait_send()

    @pl.loop(1, CHIPS)
    def _(step):
        send_tok(step).wait_send()
        relay(peer(step)[0]).wait_send()
        d1(step).wait_send()

    @pl.loop(0, NCH)
    def _(k):
        for side in range(2):
            for batch in (1, 2):
                rs1(batch, k, side).wait_send()
                rs2(batch, k, side).wait_send()
            ag1(k, side).wait_send()
            ag2(k, side).wait_send()
        for h in range(2):
            pair(k, h).wait_send()

            @pl.loop(1, CHIPS)
            def _(step):
                row_copy(k, h, step).wait_send()

    @pl.loop(0, NCH // 2)
    def _(p):
        for side in range(2):
            rs1(0, p, side).wait_send()
            rs2(0, p, side).wait_send()


def write_out(total, diag, grad_out, hess_out, diag_out):
    grad_out[...] = total[0].astype(BF)
    hess_out[...] = total[1].astype(BF)
    diag_out[...] = diag[...]


def local(tokens, probe_bits, cot_codes, cot_scales, w_gate, w_up, w_down):
    split = (ROWS, NCH, SUB)
    vm = pl.BlockSpec(memory_space=pltpu.VMEM)
    hbm = pl.BlockSpec(memory_space=pl.ANY)
    dma = pltpu.SemaphoreType.DMA
    total, diag = pl.pallas_call(
        kernel,
        out_shape=(
            jax.ShapeDtypeStruct((2, NCH * SUB, FE), F32),
            jax.ShapeDtypeStruct((1, FE), F32),
        ),
        in_specs=[vm] + [hbm] * 6,
        out_specs=[vm] * 2,
        scratch_shapes=[
            pltpu.VMEM((FE, HI2), BF),
            pltpu.VMEM((HI, FE), BF),
            pltpu.VMEM((NCH, ROWS, SUB, FE), jnp.int32),
            pltpu.VMEM((NCH, ROWS, SUB, FE), jnp.int32),
            pltpu.VMEM((FE // 32, NCH * CT), jnp.int32),
            pltpu.VMEM((FE // 32, FE), BF),
            pltpu.VMEM((NCH * CT, FE // 32), BF),
            pltpu.VMEM((NCH, CT, FE), BF),
            pltpu.VMEM((2 * CT, FE), BF),
            pltpu.VMEM((ROWS, NCH * SUB, FE), BF),
            pltpu.VMEM((NCH, CT, FE), BF),
            pltpu.VMEM((NCH, CT, HI), BF),
            pltpu.VMEM((NCH, CT, HI2), BF),
            pltpu.VMEM((NCH, CT, HI2), BF),
            pltpu.VMEM((2, NCH, HALF, HI), BF),
            pltpu.VMEM((2, NCH, HALF, HI2), BF),
            pltpu.VMEM((2, NCH, HALF, HI2), BF),
            pltpu.VMEM((2, NCH, OWN, HI), BF),
            pltpu.VMEM((2, NCH, OWN, HI2), BF),
            pltpu.VMEM((2, NCH, OWN, HI2), BF),
            pltpu.VMEM((NCH, 2, CT, HI2), BF),
            pltpu.VMEM((2, 2, CT, FH), F32),
            pltpu.VMEM((NCH, 2, CT, FH), BF),
            pltpu.VMEM((NCH, 2, CT, FH), BF),
            pltpu.VMEM((NCH, 2, CHIPS, 2 * SUB, FH), BF),
            pltpu.VMEM((NCH, 2, CHIPS, 2 * SUB, FH), BF),
            pltpu.VMEM((8, FE), F32),
            pltpu.VMEM((CHIPS, 1, FE), F32),
            pltpu.VMEM((4, 1, FE), F32),
            pltpu.VMEM((2 * CT, FH), F32),
            dma((2 * NCH + 4,)),
            dma((CHIPS,)), dma((CHIPS,)), dma((CHIPS,)), dma((CHIPS,)),
            dma((2, 2 * NCH + 2)), dma((2, 2 * NCH + 2)), dma((2, 2 * NCH + 2)), dma((2, 2 * NCH + 2)),
            dma((2, NCH)), dma((2, NCH)), dma((2, NCH)), dma((2, NCH)),
            dma((NCH, 2)), dma((NCH, 2)),
            dma((NCH, 2, CHIPS)), dma((NCH, 2, CHIPS)),
            dma((CHIPS,)), dma((CHIPS,)), dma((3,)), dma((3,)),
        ],
        compiler_params=pltpu.CompilerParams(
            collective_id=0, has_side_effects=True, vmem_limit_bytes=63 * 2**20
        ),
    )(
        tokens,
        probe_bits.reshape(split + (FE,)),
        cot_codes.reshape(split + (FE,)),
        cot_scales.T,
        w_gate,
        w_up,
        w_down,
    )
    return pl.pallas_call(
        write_out,
        out_shape=(
            jax.ShapeDtypeStruct((NCH * SUB, FE), BF),
            jax.ShapeDtypeStruct((NCH * SUB, FE), BF),
            jax.ShapeDtypeStruct((FE,), F32),
        ),
        in_specs=[vm] * 2,
        out_specs=[vm] * 3,
    )(total, diag.reshape(FE))


def solution(mesh):
    in_specs = (
        P(("rep", "row"), "col"),
        P("rep", "col"),
        P("rep", "col"),
        P("rep", "col"),
        P("col", "row"),
        P("col", "row"),
        P("row", "col"),
    )
    out_specs = (P(("rep", "row"), "col"), P(("rep", "row"), "col"), P("col"))
    return jax.shard_map(local, mesh=mesh, in_specs=in_specs, out_specs=out_specs, check_vma=False)
```

time: 112 us -> 105 us (0.938)
  local copies, waits for them, and re-layouts: 6.16 us -> 0 us
  Pallas kernels: 105 us -> 103 us
    unnamed x4 -> x0, local copies, waits for them, and re-layouts: 6.16 us -> none
    pallas_call x1 -> x2, Pallas kernels: 105 us -> 103 us  [the longest x1 101 us: local(): pl.pallas_call(kernel, out_shape=(jax.ShapeDtypeStruct((2, NCH * SUB, FE)...]
where the time goes in v2:
time: 105 us; the launch traced here: 104 us
  Pallas kernels  103 us (98%)
    pallas_call x1, Pallas kernels, local(): pl.pallas_call(kernel, out_shape=(jax.ShapeDtypeStruct((2, NCH * SUB, FE)...  101 us

profile of v2, /device:TPU:0, one launch (start us, length us, event | category | flops | bytes accessed | tf_op | source)
XLA Modules:
  0.0 103.8 jit_solution(2947975676267164282)
XLA Ops:
  0.6 101.4 %shard_map.94 = (f32[2,32,2048]{2,1,0:T(8,128)}, f32[1,2048]{1,0:T(1,128)}) custom-call(bf16[32,2048]{1,0:T(8,128)(2,1)} %tok.1, s32[16,4,8,2048]{3,2,1,0:T(8,128)} %bitcast.4, s32[16,4,8,2048]{3,2,1,0:T(8,128)} %bitcast.5, s32[64,512]{1,0:T(8,128)} %bitcast.6, bf16[2048,896]{1,0:T(8,128)(2,1)} %wg_hbm.1, bf16[2048,896]{1,0:T(8,128)(2,1)} %wu_hbm.1, ...), custom_call_target="tpu_custom_call" | custom-call | tf_op jit(solution)/shard_map/pallas_call | solution.py:483
  102.0 1.8 %shard_map.95 = (bf16[32,2048]{1,0:T(8,128)(2,1)}, bf16[32,2048]{1,0:T(8,128)(2,1)}, f32[2048]{0:T(1024)}) custom-call(f32[2,32,2048]{2,1,0:T(8,128)} %get-tuple-element.5.total, f32[2048]{0:T(1024)} %bitcast.7), custom_call_target="tpu_custom_call" | custom-call | tf_op jit(solution)/shard_map/pallas_call | solution.py:542

commit v3 on v2

--- a/solution.py
+++ b/solution.py
@@ -12,6 +12,11 @@
 F32 = jnp.float32
 REPS, ROWS, COLS = 2, 16, 4
 CHIPS = ROWS // 2
+ZS = CHIPS // 2
+NEAR = ((1, 0), (3, 0))
+MID = ((2, 0), (0, 1))
+FAR = ((1, 1), (3, 1), (2, 1))
+ALL = FAR[::-1] + MID + NEAR
 NCH = 4
 SUB = 8
 CT = ROWS * SUB
@@ -30,13 +35,12 @@
 
 def kernel(
     tok, bits_hbm, codes_hbm, scales_hbm, wg_hbm, wu_hbm, wd_hbm,
-    total, diag_out,
+    both_out, diag_out,
     w, wd, bits, codes, scales, spread, power, signs, cot, gathered, ordered,
-    part0, part1, part2, in0, in1, in2, red0, red1, red2, terms, mine,
+    part0, part1, part2, in0, in1, in2, red0, red1, red2, terms, total, mine,
     pair_out, pair_in, row_out, row_in, dsum, dbuf1, dbuf2, res,
-    load_sem, tok_send, tok_recv, sib_send, sib_recv,
-    rs1_send, rs1_recv, rs2_send, rs2_recv, ag1_send, ag1_recv, ag2_send, ag2_recv,
-    pair_send, pair_recv, row_send, row_recv, d1_send, d1_recv, d2_send, d2_recv,
+    load_sem, send_sem, tok_recv, sib_recv, rs1_recv, rs2_recv, ag1_recv, ag2_recv,
+    pair_recv, row_recv, d1_recv, d2_recv, ready,
 ):
     rep = lax.axis_index("rep")
     row = lax.axis_index("row")
@@ -49,8 +53,10 @@
     opp = lax.rem(col + 2, COLS)
     sides = (left, right)
 
-    def peer(step):
-        other = lax.rem(chip + step, CHIPS)
+    z, xh = chip // 2, lax.rem(chip, 2)
+
+    def peer(away):
+        other = lax.rem(z + away[0], ZS) * 2 + lax.rem(xh + away[1], 2)
         return other, 2 * other + core
 
     def load_bits(k):
@@ -63,9 +69,11 @@
     load_wu = pltpu.make_async_copy(wu_hbm, w.at[:, pl.ds(HI, HI)], load_sem.at[2 * NCH + 1])
     load_wd = pltpu.make_async_copy(wd_hbm, wd, load_sem.at[2 * NCH + 2])
     load_sc = pltpu.make_async_copy(scales_hbm, scales, load_sem.at[2 * NCH + 3])
+    load_tok = pltpu.make_async_copy(tok, gathered.at[row], load_sem.at[2 * NCH + 4])
     load_sc.start()
     load_codes(0).start()
     load_codes(1).start()
+    load_tok.start()
     load_wd.start()
     load_codes(2).start()
     load_codes(3).start()
@@ -76,41 +84,58 @@
         load_bits(k).start()
 
     barrier = pltpu.get_barrier_semaphore()
+
+    def tell(sem, where):
+        pl.semaphore_signal(sem, inc=1, device_id=where, device_id_type=MESH)
+
+    opposite_row = peer((0, 1))[1]
     for side in sides:
-        pl.semaphore_signal(barrier, inc=1, device_id={"col": side}, device_id_type=MESH)
-    pl.semaphore_signal(barrier, inc=1, device_id={"row": sib}, device_id_type=MESH)
-    for other_row in (row, sib):
-        pl.semaphore_signal(
-            barrier, inc=1, device_id={"rep": 1 - rep, "row": other_row}, device_id_type=MESH
+        tell(barrier, {"col": side})
+    tell(barrier, {"row": sib})
+    for away in NEAR:
+        tell(barrier, {"row": peer(away)[1]})
+    for other_row in (row, sib, opposite_row):
+        tell(barrier, {"rep": 1 - rep, "row": other_row})
+
+    def enter_first():
+        pl.semaphore_wait(barrier, 8)
+        for away in NEAR:
+            tell(ready.at[0], {"row": peer(away)[1]})
+        tell(ready.at[0], {"rep": 1 - rep})
+
+    def enter_second():
+        pl.semaphore_wait(ready.at[0], 3)
+        tell(ready.at[1], {"row": opposite_row})
+
+    def enter_third():
+        pl.semaphore_wait(ready.at[1], 1)
+
+    def remote(src, dst, recv, where):
+        return pltpu.make_async_remote_copy(
+            src_ref=src, dst_ref=dst, send_sem=send_sem.at[0], recv_sem=recv, device_id=where, device_id_type=MESH
         )
-    for step in range(1, CHIPS):
-        pl.semaphore_signal(barrier, inc=1, device_id={"row": peer(step)[1]}, device_id_type=MESH)
-    pl.semaphore_wait(barrier, 5 + CHIPS - 1)
-
-    def remote(src, dst, send, recv, where):
-        return pltpu.make_async_remote_copy(
-            src_ref=src, dst_ref=dst, send_sem=send, recv_sem=recv, device_id=where, device_id_type=MESH
-        )
-
-    def send_tok(step):
-        other, where = peer(step)
-        return remote(tok, gathered.at[row], tok_send.at[other], tok_recv.at[chip], {"row": where})
-
-    def recv_tok(other):
-        block = gathered.at[2 * other + core]
-        return remote(block, block, tok_send.at[other], tok_recv.at[other], {"row": sib})
-
-    def own_to_sib():
-        return remote(tok, gathered.at[row], sib_send.at[chip], sib_recv.at[chip], {"row": sib})
-
-    def relay(other):
-        block = gathered.at[2 * other + core]
-        return remote(block, block, sib_send.at[other], sib_recv.at[other], {"row": sib})
-
-    own_to_sib().start()
-    for step in range(1, CHIPS):
-        send_tok(step).start()
-    gathered[row] = tok[...]
+
+    def arrived(block, recv):
+        remote(block, block, recv, {"row": sib}).wait_recv()
+
+    def sent(block):
+        remote(block, block, tok_recv.at[0], {"row": sib}).wait_send()
+
+    across = (0, 1)
+    column = NEAR + ((2, 0),)
+
+    def send_tok(block_row, where, recv):
+        block = gathered.at[block_row]
+        return remote(block, block, recv, {"row": where})
+
+    def own_tok(away):
+        return send_tok(row, peer(away)[1], tok_recv.at[0 if away == across else 1])
+
+    def onward_tok(away):
+        return send_tok(opposite_row, peer(away)[1], tok_recv.at[1])
+
+    def share_tok(block_row):
+        return send_tok(block_row, sib, sib_recv.at[0])
 
     lanes = lax.broadcasted_iota(jnp.int32, spread.shape, 1) // 32
     spread[...] = (lanes == lax.broadcasted_iota(jnp.int32, spread.shape, 0)).astype(F32).astype(BF)
@@ -127,31 +152,31 @@
         part, inn, _, n, base = batches[batch]
         ks = pl.ds(k * n, n)
         src = part.at[ks, pl.ds(aligned(OWN * opp + HALF * side, HALF), HALF)]
-        return remote(
-            src, inn.at[side, ks], rs1_send.at[side, base + k], rs1_recv.at[side, base + k], {"col": sides[side]}
-        )
+        return remote(src, inn.at[side, ks], rs1_recv.at[base + k], {"col": sides[side]})
 
     def rs2(batch, k, side):
         part, _, red, n, base = batches[batch]
         ks = pl.ds(k * n, n)
         src = part.at[ks, pl.ds(aligned(OWN * sides[side], OWN), OWN)]
-        return remote(
-            src, red.at[side, ks], rs2_send.at[side, base + k], rs2_recv.at[side, base + k], {"col": sides[side]}
-        )
+        return remote(src, red.at[side, ks], rs2_recv.at[base + k], {"col": sides[side]})
 
     def start_rs1(batch, k):
         for side in range(2):
             rs1(batch, k, side).start()
 
     def fold(batch, k):
-        part, inn, _, n, _ = batches[batch]
+        part, inn, _, n, base = batches[batch]
+        arrived(inn.at[:, pl.ds(k * n, n)], rs1_recv.at[base + k])
         for side in range(2):
-            rs1(batch, k, side).wait_recv()
             rows = pl.ds(aligned(OWN * sides[side] + HALF * side, HALF), HALF)
             for i in range(n):
                 at = k * n + i
                 part[at, rows] = (part[at, rows].astype(F32) + inn[side, at].astype(F32)).astype(BF)
             rs2(batch, k, side).start()
+
+    def folded(batch, k):
+        _, _, red, n, base = batches[batch]
+        arrived(red.at[:, pl.ds(k * n, n)], rs2_recv.at[base + k])
 
     def down(p):
         for i in range(2):
@@ -168,14 +193,12 @@
             )
             cot[:, cols] = (value * wide).astype(BF)
 
-        @pl.when(p == 0)
-        def _():
+        if p == 0:
             load_wd.wait()
 
         part0[pl.ds(2 * p, 2)] = (
             lax.dot_general(cot[...], wd[...], NT, preferred_element_type=F32).astype(BF).reshape(2, CT, HI)
         )
-        start_rs1(0, p)
 
     def tangent(k):
         load_bits(k).wait()
@@ -193,17 +216,21 @@
         part2[k] = jnp.dot(ordered[k], w[...], preferred_element_type=F32).astype(BF)
         start_rs1(2, k)
 
+    def onward_tokens():
+        arrived(gathered.at[opposite_row], tok_recv.at[0])
+        for away in column:
+            onward_tok(away).start()
+        share_tok(opposite_row).start()
+
     def gather_tokens():
-        @pl.loop(1, CHIPS)
-        def _(step):
-            other = peer(step)[0]
-            recv_tok(other).wait_recv()
-            relay(other).start()
+        arrived(gathered.at[pl.ds(0, 6)], tok_recv.at[1])
+        for away in column:
+            other, where = peer(away)
+            share_tok(where).start()
+            share_tok(peer((away[0], 1))[1]).start()
 
     def order_tokens():
-        @pl.loop(0, CHIPS)
-        def _(other):
-            relay(other).wait_recv()
+        arrived(gathered.at[pl.ds(0, CHIPS)], sib_recv.at[0])
 
         @pl.loop(0, CHIPS)
         def _(q):
@@ -215,17 +242,31 @@
                 ordered[2 * h, out] = jnp.concatenate([even[:SUB], odd[:SUB]], axis=0).astype(BF)
                 ordered[2 * h + 1, out] = jnp.concatenate([even[SUB:], odd[SUB:]], axis=0).astype(BF)
 
-    @pl.loop(0, 2)
-    def _(p):
-        down(p)
+    down(0)
+    enter_first()
+    start_rs1(0, 0)
+    load_tok.wait()
+    for away in NEAR:
+        own_tok(away).start()
+    share_tok(row).start()
+    down(1)
+    start_rs1(0, 1)
+    enter_second()
+    own_tok(across).start()
+    own_tok((2, 0)).start()
+    fold(0, 0)
 
     @pl.loop(0, NCH)
     def _(s):
-        @pl.when(s < 2)
-        def _():
-            fold(0, s)
-
         tangent(s)
+
+        @pl.when(s == 0)
+        def _():
+            fold(0, 1)
+
+        @pl.when(s == 1)
+        def _():
+            onward_tokens()
 
         @pl.when(s >= 2)
         def _():
@@ -233,6 +274,7 @@
 
     gather_tokens()
     order_tokens()
+    enter_third()
 
     @pl.loop(0, NCH)
     def _(s):
@@ -250,22 +292,20 @@
 
     def ag1(k, side):
         block = terms.at[k, :, pl.ds(aligned(OWN * col, OWN), OWN)]
-        return remote(block, block, ag1_send.at[side, k], ag1_recv.at[side, k], {"col": sides[side]})
+        return remote(block, block, ag1_recv.at[k], {"col": sides[side]})
 
     def ag2(k, side):
         rows = pl.ds(aligned(OWN * sides[1 - side] + HALF * side, HALF), HALF)
         block = terms.at[k, :, rows]
-        return remote(block, block, ag2_send.at[side, k], ag2_recv.at[side, k], {"col": sides[side]})
+        return remote(block, block, ag2_recv.at[k], {"col": sides[side]})
 
     def work_terms(k):
-        for side in range(2):
-            rs2(1, k, side).wait_recv()
-            rs2(2, k, side).wait_recv()
+        folded(1, k)
+        folded(2, k)
 
         @pl.when(lax.rem(k, 2) == 0)
         def _():
-            for side in range(2):
-                rs2(0, k // 2, side).wait_recv()
+            folded(0, k // 2)
 
         rows = pl.ds(aligned(OWN * col, OWN), OWN)
 
@@ -294,33 +334,21 @@
             ag1(k, side).start()
 
     def forward_terms(k):
+        arrived(terms.at[k, :, pl.ds(0, 2 * OWN)], ag1_recv.at[k])
         for side in range(2):
-            ag1(k, side).wait_recv()
             ag2(k, side).start()
 
     def pair(k, h):
-        return remote(
-            pair_out.at[k, h], pair_in.at[k, h], pair_send.at[k, h], pair_recv.at[k, h], {"row": sib}
-        )
-
-    def row_copy(k, h, step):
-        other, where = peer(step)
-        return remote(
-            row_out.at[k, h, other], row_in.at[k, h, chip],
-            row_send.at[k, h, other], row_recv.at[k, h, chip], {"row": where},
-        )
-
-    def row_wait(k, h, other):
-        return remote(
-            row_out.at[k, h, other], row_in.at[k, h, other],
-            row_send.at[k, h, other], row_recv.at[k, h, other], {"row": sib},
-        )
+        return remote(pair_out.at[k, h], pair_in.at[k, h], pair_recv.at[k, h], {"row": sib})
+
+    def row_copy(k, h, away):
+        other, where = peer(away)
+        return remote(row_out.at[k, h, other], row_in.at[k, h, chip], row_recv.at[k, h], {"row": where})
 
     dsum[...] = jnp.zeros_like(dsum)
 
     def backward(k):
-        for side in range(2):
-            ag2(k, side).wait_recv()
+        arrived(terms.at[k, :, pl.ds(0, OWN)], ag2_recv.at[k])
         slot = lax.rem(k, 2)
 
         @pl.loop(0, 2)
@@ -359,19 +387,15 @@
                 rows = pl.ds(aligned(2 * SUB * m, 2 * SUB), 2 * SUB)
                 row_out[k, h, m] = (mine[slot, h, rows] + pair_in[k, h, rows].astype(F32)).astype(BF)
 
-            @pl.loop(1, CHIPS)
-            def _(step):
-                row_copy(k, h, step).start()
+            for away in ALL:
+                row_copy(k, h, away).start()
 
             row_in[k, h, chip] = row_out[k, h, chip]
 
     def finish(k):
         rows = pl.ds(aligned(SUB * k, SUB), SUB)
         for h in range(2):
-
-            @pl.loop(1, CHIPS)
-            def _(step):
-                row_wait(k, h, peer(step)[0]).wait_recv()
+            arrived(row_in.at[k, h, pl.ds(0, CHIPS - 1)], row_recv.at[k, h])
 
             total_k = row_in[k, h, 0].astype(F32)
             for m in range(1, CHIPS):
@@ -380,18 +404,14 @@
             total[0, rows, cols] = total_k[:SUB]
             total[1, rows, cols] = total_k[SUB:]
 
-    def d1(step):
-        other, where = peer(step)
-        return remote(dbuf1.at[chip], dbuf1.at[chip], d1_send.at[other], d1_recv.at[chip], {"row": where})
-
-    def d1_wait(other):
-        return remote(dbuf1.at[other], dbuf1.at[other], d1_send.at[other], d1_recv.at[other], {"row": sib})
+    def d1(away):
+        return remote(dbuf1.at[chip], dbuf1.at[chip], d1_recv.at[0], {"row": peer(away)[1]})
 
     quad = 2 * rep + core
 
     def d2(which):
         where = ({"row": sib}, {"rep": 1 - rep}, {"rep": 1 - rep, "row": sib})[which]
-        return remote(dbuf2.at[quad], dbuf2.at[quad], d2_send.at[which], d2_recv.at[which], where)
+        return remote(dbuf2.at[quad], dbuf2.at[quad], d2_recv.at[0], where)
 
     @pl.loop(0, NCH + 4)
     def _(s):
@@ -418,13 +438,12 @@
         @pl.when(s == NCH + 1)
         def _():
             dbuf1[chip] = jnp.sum(dsum[...], axis=0, keepdims=True)
-            for step in range(1, CHIPS):
-                d1(step).start()
+            for away in ALL:
+                d1(away).start()
 
         @pl.when(s == NCH + 2)
         def _():
-            for step in range(1, CHIPS):
-                d1_wait(peer(step)[0]).wait_recv()
+            arrived(dbuf1.at[pl.ds(0, CHIPS - 1)], d1_recv.at[0])
             dbuf2[quad] = jnp.sum(dbuf1[...], axis=0)
             for which in range(3):
                 d2(which).start()
@@ -433,45 +452,24 @@
         def _():
             finish(s - 4)
 
-    for which in range(3):
-        d2(which).wait_recv()
+    both_out[...] = total[...].astype(BF)
+    arrived(dbuf2.at[pl.ds(0, 3)], d2_recv.at[0])
     diag_out[...] = jnp.sum(dbuf2[...], axis=0) * (1.0 / (REPS * ROWS * NCH * SUB))
 
-    own_to_sib().wait_send()
-    for which in range(3):
-        d2(which).wait_send()
-
-    @pl.loop(1, CHIPS)
-    def _(step):
-        send_tok(step).wait_send()
-        relay(peer(step)[0]).wait_send()
-        d1(step).wait_send()
-
-    @pl.loop(0, NCH)
-    def _(k):
-        for side in range(2):
-            for batch in (1, 2):
-                rs1(batch, k, side).wait_send()
-                rs2(batch, k, side).wait_send()
-            ag1(k, side).wait_send()
-            ag2(k, side).wait_send()
-        for h in range(2):
-            pair(k, h).wait_send()
-
-            @pl.loop(1, CHIPS)
-            def _(step):
-                row_copy(k, h, step).wait_send()
-
-    @pl.loop(0, NCH // 2)
-    def _(p):
-        for side in range(2):
-            rs1(0, p, side).wait_send()
-            rs2(0, p, side).wait_send()
+    for block in (in0, in1, in2, red0, red1, red2, pair_out):
+        sent(block)
+    sent(gathered.at[pl.ds(0, CHIPS - 1)])
+    sent(gathered.at[pl.ds(0, CHIPS)])
+    sent(terms.at[:, :, pl.ds(0, 2 * OWN)])
+    sent(terms.at[:, :, pl.ds(0, OWN)])
+    sent(row_out.at[:, :, pl.ds(0, CHIPS - 1)])
+    sent(dbuf1.at[pl.ds(0, CHIPS - 1)])
+    sent(dbuf2.at[pl.ds(0, 3)])
 
 
 def write_out(total, diag, grad_out, hess_out, diag_out):
-    grad_out[...] = total[0].astype(BF)
-    hess_out[...] = total[1].astype(BF)
+    grad_out[...] = total[0]
+    hess_out[...] = total[1]
     diag_out[...] = diag[...]
 
 
@@ -483,10 +481,10 @@
     total, diag = pl.pallas_call(
         kernel,
         out_shape=(
-            jax.ShapeDtypeStruct((2, NCH * SUB, FE), F32),
+            jax.ShapeDtypeStruct((2, NCH * SUB, FE), BF),
             jax.ShapeDtypeStruct((1, FE), F32),
         ),
-        in_specs=[vm] + [hbm] * 6,
+        in_specs=[hbm] * 7,
         out_specs=[vm] * 2,
         scratch_shapes=[
             pltpu.VMEM((FE, HI2), BF),
@@ -510,6 +508,7 @@
             pltpu.VMEM((2, NCH, OWN, HI2), BF),
             pltpu.VMEM((2, NCH, OWN, HI2), BF),
             pltpu.VMEM((NCH, 2, CT, HI2), BF),
+            pltpu.VMEM((2, NCH * SUB, FE), F32),
             pltpu.VMEM((2, 2, CT, FH), F32),
             pltpu.VMEM((NCH, 2, CT, FH), BF),
             pltpu.VMEM((NCH, 2, CT, FH), BF),
@@ -519,13 +518,13 @@
             pltpu.VMEM((CHIPS, 1, FE), F32),
             pltpu.VMEM((4, 1, FE), F32),
             pltpu.VMEM((2 * CT, FH), F32),
-            dma((2 * NCH + 4,)),
-            dma((CHIPS,)), dma((CHIPS,)), dma((CHIPS,)), dma((CHIPS,)),
-            dma((2, 2 * NCH + 2)), dma((2, 2 * NCH + 2)), dma((2, 2 * NCH + 2)), dma((2, 2 * NCH + 2)),
-            dma((2, NCH)), dma((2, NCH)), dma((2, NCH)), dma((2, NCH)),
+            dma((2 * NCH + 5,)), dma((1,)),
+            dma((2,)), dma((1,)),
+            dma((2 * NCH + 2,)), dma((2 * NCH + 2,)),
+            dma((NCH,)), dma((NCH,)),
             dma((NCH, 2)), dma((NCH, 2)),
-            dma((NCH, 2, CHIPS)), dma((NCH, 2, CHIPS)),
-            dma((CHIPS,)), dma((CHIPS,)), dma((3,)), dma((3,)),
+            dma((1,)), dma((1,)),
+            pltpu.SemaphoreType.REGULAR((2,)),
         ],
         compiler_params=pltpu.CompilerParams(
             collective_id=0, has_side_effects=True, vmem_limit_bytes=63 * 2**20

time: 105 us -> 99.4 us (0.947); the launches traced: 104 us -> 99.3 us
  Pallas kernels: 103 us -> 98.7 us
    pallas_call x1, Pallas kernels: 101 us -> 97 us  [local(): pl.pallas_call(kernel, out_shape=(jax.ShapeDtypeStruct((2, NCH * SUB, FE)...]
where the time goes in v3:
time: 99.4 us; the launch traced here: 99.3 us
  Pallas kernels  98.7 us (99%)
    pallas_call x1, Pallas kernels, local(): pl.pallas_call(kernel, out_shape=(jax.ShapeDtypeStruct((2, NCH * SUB, FE)...  97 us

profile of v3, /device:TPU:0, one launch (start us, length us, event | category | flops | bytes accessed | tf_op | source)
XLA Modules:
  0.0 99.3 jit_solution(10186804887585009053)
XLA Ops:
  0.6 97.0 %shard_map.94 = (bf16[2,32,2048]{2,1,0:T(8,128)(2,1)}, f32[1,2048]{1,0:T(1,128)}) custom-call(bf16[32,2048]{1,0:T(8,128)(2,1)} %tok.1, s32[16,4,8,2048]{3,2,1,0:T(8,128)} %bitcast.4, s32[16,4,8,2048]{3,2,1,0:T(8,128)} %bitcast.5, s32[64,512]{1,0:T(8,128)} %bitcast.6, bf16[2048,896]{1,0:T(8,128)(2,1)} %wg_hbm.1, bf16[2048,896]{1,0:T(8,128)(2,1)} %wu_hbm.1, ...), custom_call_target="tpu_custom_call" | custom-call | tf_op jit(solution)/shard_map/pallas_call | solution.py:481
  97.6 1.7 %shard_map.95 = (bf16[32,2048]{1,0:T(8,128)(2,1)}, bf16[32,2048]{1,0:T(8,128)(2,1)}, f32[2048]{0:T(1024)}) custom-call(bf16[2,32,2048]{2,1,0:T(8,128)(2,1)} %get-tuple-element.5.total, f32[2048]{0:T(1024)} %bitcast.7), custom_call_target="tpu_custom_call" | custom-call | tf_op jit(solution)/shard_map/pallas_call | solution.py:541

commit v4 on v3

--- a/solution.py
+++ b/solution.py
@@ -290,9 +290,10 @@
 
     fold(2, 2)
 
-    def ag1(k, side):
-        block = terms.at[k, :, pl.ds(aligned(OWN * col, OWN), OWN)]
-        return remote(block, block, ag1_recv.at[k], {"col": sides[side]})
+    def ag1(k, side, later):
+        half = 1 - side if later else side
+        block = terms.at[k, :, pl.ds(aligned(OWN * col + HALF * half, HALF), HALF)]
+        return remote(block, block, ag1_recv.at[later, k], {"col": sides[side]})
 
     def ag2(k, side):
         rows = pl.ds(aligned(OWN * sides[1 - side] + HALF * side, HALF), HALF)
@@ -330,11 +331,12 @@
                 down_back * (up_tan * first + up_pre * second * gate_tan)
             ).astype(BF)
             terms[k, 1, rows, pl.ds(HI + start, 128)] = (down_first * gate_tan).astype(BF)
-        for side in range(2):
-            ag1(k, side).start()
+        for later in range(2):
+            for side in range(2):
+                ag1(k, side, later).start()
 
     def forward_terms(k):
-        arrived(terms.at[k, :, pl.ds(0, 2 * OWN)], ag1_recv.at[k])
+        arrived(terms.at[k, :, pl.ds(0, OWN)], ag1_recv.at[0, k])
         for side in range(2):
             ag2(k, side).start()
 
@@ -348,6 +350,7 @@
     dsum[...] = jnp.zeros_like(dsum)
 
     def backward(k):
+        arrived(terms.at[k, :, pl.ds(0, OWN)], ag1_recv.at[1, k])
         arrived(terms.at[k, :, pl.ds(0, OWN)], ag2_recv.at[k])
         slot = lax.rem(k, 2)
 
@@ -413,7 +416,7 @@
         where = ({"row": sib}, {"rep": 1 - rep}, {"rep": 1 - rep, "row": sib})[which]
         return remote(dbuf2.at[quad], dbuf2.at[quad], d2_recv.at[0], where)
 
-    @pl.loop(0, NCH + 4)
+    @pl.loop(0, NCH + 3)
     def _(s):
         @pl.when(s < NCH)
         def _():
@@ -423,34 +426,34 @@
         def _():
             fold(2, NCH - 1)
 
+        @pl.when(jnp.logical_and(s >= 2, s < NCH + 2))
+        def _():
+            send_rows(s - 2)
+
         @pl.when(jnp.logical_and(s >= 1, s < NCH + 1))
         def _():
-            forward_terms(s - 1)
-
-        @pl.when(jnp.logical_and(s >= 3, s < NCH + 3))
-        def _():
-            send_rows(s - 3)
-
-        @pl.when(jnp.logical_and(s >= 2, s < NCH + 2))
-        def _():
-            backward(s - 2)
-
-        @pl.when(s == NCH + 1)
+            backward(s - 1)
+
+        @pl.when(s < NCH)
+        def _():
+            forward_terms(s)
+
+        @pl.when(s == NCH)
         def _():
             dbuf1[chip] = jnp.sum(dsum[...], axis=0, keepdims=True)
             for away in ALL:
                 d1(away).start()
 
-        @pl.when(s == NCH + 2)
+        @pl.when(s == NCH + 1)
         def _():
             arrived(dbuf1.at[pl.ds(0, CHIPS - 1)], d1_recv.at[0])
             dbuf2[quad] = jnp.sum(dbuf1[...], axis=0)
             for which in range(3):
                 d2(which).start()
 
-        @pl.when(s >= 4)
-        def _():
-            finish(s - 4)
+        @pl.when(s >= 3)
+        def _():
+            finish(s - 3)
 
     both_out[...] = total[...].astype(BF)
     arrived(dbuf2.at[pl.ds(0, 3)], d2_recv.at[0])
@@ -521,7 +524,7 @@
             dma((2 * NCH + 5,)), dma((1,)),
             dma((2,)), dma((1,)),
             dma((2 * NCH + 2,)), dma((2 * NCH + 2,)),
-            dma((NCH,)), dma((NCH,)),
+            dma((2, NCH)), dma((NCH,)),
             dma((NCH, 2)), dma((NCH, 2)),
             dma((1,)), dma((1,)),
             pltpu.SemaphoreType.REGULAR((2,)),

time: 99.4 us -> 96.4 us (0.970)
  Pallas kernels: 98.7 us -> 95.6 us
    pallas_call x1, Pallas kernels: 97 us -> 94 us  [local(): pl.pallas_call(kernel, out_shape=(jax.ShapeDtypeStruct((2, NCH * SUB, FE)...]
where the time goes in v4:
time: 96.4 us; the launch traced here: 96.3 us
  Pallas kernels  95.6 us (99%)
    pallas_call x1, Pallas kernels, local(): pl.pallas_call(kernel, out_shape=(jax.ShapeDtypeStruct((2, NCH * SUB, FE)...  94 us

profile of v4, /device:TPU:0, one launch (start us, length us, event | category | flops | bytes accessed | tf_op | source)
XLA Modules:
  0.0 96.3 jit_solution(12459754128718670997)
XLA Ops:
  0.6 94.0 %shard_map.94 = (bf16[2,32,2048]{2,1,0:T(8,128)(2,1)}, f32[1,2048]{1,0:T(1,128)}) custom-call(bf16[32,2048]{1,0:T(8,128)(2,1)} %tok.1, s32[16,4,8,2048]{3,2,1,0:T(8,128)} %bitcast.4, s32[16,4,8,2048]{3,2,1,0:T(8,128)} %bitcast.5, s32[64,512]{1,0:T(8,128)} %bitcast.6, bf16[2048,896]{1,0:T(8,128)(2,1)} %wg_hbm.1, bf16[2048,896]{1,0:T(8,128)(2,1)} %wu_hbm.1, ...), custom_call_target="tpu_custom_call" | custom-call | tf_op jit(solution)/shard_map/pallas_call | solution.py:484
  94.6 1.7 %shard_map.95 = (bf16[32,2048]{1,0:T(8,128)(2,1)}, bf16[32,2048]{1,0:T(8,128)(2,1)}, f32[2048]{0:T(1024)}) custom-call(bf16[2,32,2048]{2,1,0:T(8,128)(2,1)} %get-tuple-element.5.total, f32[2048]{0:T(1024)} %bitcast.7), custom_call_target="tpu_custom_call" | custom-call | tf_op jit(solution)/shard_map/pallas_call | solution.py:544

commit v5 on v4

--- a/solution.py
+++ b/solution.py
@@ -94,11 +94,12 @@
     tell(barrier, {"row": sib})
     for away in NEAR:
         tell(barrier, {"row": peer(away)[1]})
-    for other_row in (row, sib, opposite_row):
+    opposite_sib = opposite_row + 1 - 2 * core
+    for other_row in (row, sib, opposite_row, opposite_sib):
         tell(barrier, {"rep": 1 - rep, "row": other_row})
 
     def enter_first():
-        pl.semaphore_wait(barrier, 8)
+        pl.semaphore_wait(barrier, 9)
         for away in NEAR:
             tell(ready.at[0], {"row": peer(away)[1]})
         tell(ready.at[0], {"rep": 1 - rep})
@@ -119,23 +120,26 @@
         remote(block, block, recv, {"row": sib}).wait_recv()
 
     def sent(block):
-        remote(block, block, tok_recv.at[0], {"row": sib}).wait_send()
+        remote(block, block, sib_recv.at[0], {"row": sib}).wait_send()
 
     across = (0, 1)
     column = NEAR + ((2, 0),)
 
-    def send_tok(block_row, where, recv):
-        block = gathered.at[block_row]
+    def tok_rows(h):
+        return pl.ds(2 * SUB * h, 2 * SUB)
+
+    def send_tok(block_row, h, where, recv):
+        block = gathered.at[block_row, tok_rows(h)]
         return remote(block, block, recv, {"row": where})
 
-    def own_tok(away):
-        return send_tok(row, peer(away)[1], tok_recv.at[0 if away == across else 1])
-
-    def onward_tok(away):
-        return send_tok(opposite_row, peer(away)[1], tok_recv.at[1])
-
-    def share_tok(block_row):
-        return send_tok(block_row, sib, sib_recv.at[0])
+    def own_tok(away, h):
+        return send_tok(row, h, peer(away)[1], tok_recv.at[0 if away == across else 1, h])
+
+    def onward_tok(away, h):
+        return send_tok(opposite_row, h, peer(away)[1], tok_recv.at[1, h])
+
+    def share_tok(block_row, h):
+        return send_tok(block_row, h, sib, sib_recv.at[h])
 
     lanes = lax.broadcasted_iota(jnp.int32, spread.shape, 1) // 32
     spread[...] = (lanes == lax.broadcasted_iota(jnp.int32, spread.shape, 0)).astype(F32).astype(BF)
@@ -216,45 +220,42 @@
         part2[k] = jnp.dot(ordered[k], w[...], preferred_element_type=F32).astype(BF)
         start_rs1(2, k)
 
-    def onward_tokens():
-        arrived(gathered.at[opposite_row], tok_recv.at[0])
+    def onward_tokens(h):
+        arrived(gathered.at[opposite_row, tok_rows(h)], tok_recv.at[0, h])
         for away in column:
-            onward_tok(away).start()
-        share_tok(opposite_row).start()
-
-    def gather_tokens():
-        arrived(gathered.at[pl.ds(0, 6)], tok_recv.at[1])
+            onward_tok(away, h).start()
+        share_tok(opposite_row, h).start()
+
+    def gather_tokens(h):
+        arrived(gathered.at[pl.ds(0, 6), tok_rows(h)], tok_recv.at[1, h])
         for away in column:
             other, where = peer(away)
-            share_tok(where).start()
-            share_tok(peer((away[0], 1))[1]).start()
-
-    def order_tokens():
-        arrived(gathered.at[pl.ds(0, CHIPS)], sib_recv.at[0])
+            share_tok(where, h).start()
+            share_tok(peer((away[0], 1))[1], h).start()
+
+    def order_tokens(h):
+        arrived(gathered.at[pl.ds(0, CHIPS), tok_rows(h)], sib_recv.at[h])
 
         @pl.loop(0, CHIPS)
         def _(q):
-            for h in range(NCH // 2):
-                rows = pl.ds(2 * SUB * h, 2 * SUB)
-                even = gathered[2 * q, rows].astype(F32)
-                odd = gathered[2 * q + 1, rows].astype(F32)
-                out = pl.ds(aligned(2 * SUB * q, 2 * SUB), 2 * SUB)
-                ordered[2 * h, out] = jnp.concatenate([even[:SUB], odd[:SUB]], axis=0).astype(BF)
-                ordered[2 * h + 1, out] = jnp.concatenate([even[SUB:], odd[SUB:]], axis=0).astype(BF)
+            even = gathered[2 * q, tok_rows(h)].astype(F32)
+            odd = gathered[2 * q + 1, tok_rows(h)].astype(F32)
+            out = pl.ds(aligned(2 * SUB * q, 2 * SUB), 2 * SUB)
+            ordered[2 * h, out] = jnp.concatenate([even[:SUB], odd[:SUB]], axis=0).astype(BF)
+            ordered[2 * h + 1, out] = jnp.concatenate([even[SUB:], odd[SUB:]], axis=0).astype(BF)
 
     down(0)
     enter_first()
     start_rs1(0, 0)
     load_tok.wait()
     for away in NEAR:
-        own_tok(away).start()
-    share_tok(row).start()
+        own_tok(away, 0).start()
+    share_tok(row, 0).start()
     down(1)
     start_rs1(0, 1)
     enter_second()
-    own_tok(across).start()
-    own_tok((2, 0)).start()
-    fold(0, 0)
+    own_tok(across, 0).start()
+    own_tok((2, 0), 0).start()
 
     @pl.loop(0, NCH)
     def _(s):
@@ -262,23 +263,42 @@
 
         @pl.when(s == 0)
         def _():
+            fold(0, 0)
             fold(0, 1)
 
         @pl.when(s == 1)
         def _():
-            onward_tokens()
+            onward_tokens(0)
+            for away in (across,) + column:
+                own_tok(away, 1).start()
+            share_tok(row, 1).start()
+
+        @pl.when(s == 3)
+        def _():
+            gather_tokens(0)
+            onward_tokens(1)
 
         @pl.when(s >= 2)
         def _():
             fold(1, s - 2)
 
-    gather_tokens()
-    order_tokens()
-    enter_third()
+    order_tokens(0)
 
     @pl.loop(0, NCH)
     def _(s):
+        @pl.when(s == 2)
+        def _():
+            order_tokens(1)
+
         primal(s)
+
+        @pl.when(s == 0)
+        def _():
+            enter_third()
+
+        @pl.when(s == 1)
+        def _():
+            gather_tokens(1)
 
         @pl.when(s < 2)
         def _():
@@ -408,13 +428,17 @@
             total[1, rows, cols] = total_k[SUB:]
 
     def d1(away):
-        return remote(dbuf1.at[chip], dbuf1.at[chip], d1_recv.at[0], {"row": peer(away)[1]})
-
-    quad = 2 * rep + core
-
-    def d2(which):
-        where = ({"row": sib}, {"rep": 1 - rep}, {"rep": 1 - rep, "row": sib})[which]
-        return remote(dbuf2.at[quad], dbuf2.at[quad], d2_recv.at[0], where)
+        return remote(dbuf1.at[z], dbuf1.at[z], d1_recv.at[0], {"row": peer(away)[1]})
+
+    octet = 4 * rep + 2 * xh + core
+
+    def d2():
+        block = dbuf2.at[octet]
+        for other_row in (opposite_row, opposite_sib):
+            yield remote(block, block, d2_recv.at[0], {"row": other_row})
+        for other_row in (row, sib, opposite_row, opposite_sib):
+            yield remote(block, block, d2_recv.at[0], {"rep": 1 - rep, "row": other_row})
+        yield remote(block, block, d2_recv.at[0], {"row": sib})
 
     @pl.loop(0, NCH + 3)
     def _(s):
@@ -440,23 +464,23 @@
 
         @pl.when(s == NCH)
         def _():
-            dbuf1[chip] = jnp.sum(dsum[...], axis=0, keepdims=True)
-            for away in ALL:
+            dbuf1[z] = jnp.sum(dsum[...], axis=0, keepdims=True)
+            for away in column[::-1]:
                 d1(away).start()
 
         @pl.when(s == NCH + 1)
         def _():
-            arrived(dbuf1.at[pl.ds(0, CHIPS - 1)], d1_recv.at[0])
-            dbuf2[quad] = jnp.sum(dbuf1[...], axis=0)
-            for which in range(3):
-                d2(which).start()
+            arrived(dbuf1.at[pl.ds(0, ZS - 1)], d1_recv.at[0])
+            dbuf2[octet] = jnp.sum(dbuf1[...], axis=0)
+            for copy in d2():
+                copy.start()
 
         @pl.when(s >= 3)
         def _():
             finish(s - 3)
 
     both_out[...] = total[...].astype(BF)
-    arrived(dbuf2.at[pl.ds(0, 3)], d2_recv.at[0])
+    arrived(dbuf2.at[pl.ds(0, 7)], d2_recv.at[0])
     diag_out[...] = jnp.sum(dbuf2[...], axis=0) * (1.0 / (REPS * ROWS * NCH * SUB))
 
     for block in (in0, in1, in2, red0, red1, red2, pair_out):
@@ -466,8 +490,8 @@
     sent(terms.at[:, :, pl.ds(0, 2 * OWN)])
     sent(terms.at[:, :, pl.ds(0, OWN)])
     sent(row_out.at[:, :, pl.ds(0, CHIPS - 1)])
-    sent(dbuf1.at[pl.ds(0, CHIPS - 1)])
-    sent(dbuf2.at[pl.ds(0, 3)])
+    sent(dbuf1.at[pl.ds(0, ZS - 1)])
+    sent(dbuf2.at[pl.ds(0, 7)])
 
 
 def write_out(total, diag, grad_out, hess_out, diag_out):
@@ -518,11 +542,11 @@
             pltpu.VMEM((NCH, 2, CHIPS, 2 * SUB, FH), BF),
             pltpu.VMEM((NCH, 2, CHIPS, 2 * SUB, FH), BF),
             pltpu.VMEM((8, FE), F32),
-            pltpu.VMEM((CHIPS, 1, FE), F32),
-            pltpu.VMEM((4, 1, FE), F32),
+            pltpu.VMEM((ZS, 1, FE), F32),
+            pltpu.VMEM((8, 1, FE), F32),
             pltpu.VMEM((2 * CT, FH), F32),
             dma((2 * NCH + 5,)), dma((1,)),
-            dma((2,)), dma((1,)),
+            dma((2, 2)), dma((2,)),
             dma((2 * NCH + 2,)), dma((2 * NCH + 2,)),
             dma((2, NCH)), dma((NCH,)),
             dma((NCH, 2)), dma((NCH, 2)),

time: 96.4 us -> 96.5 us (level)
  no operation moved by 1% of the time
where the time goes in v5:
time: 96.5 us; the launch traced here: 96.3 us
  Pallas kernels  95.7 us (99%)
    pallas_call x1, Pallas kernels, local(): pl.pallas_call(kernel, out_shape=(jax.ShapeDtypeStruct((2, NCH * SUB, FE)...  94 us

profile of v5, /device:TPU:0, one launch (start us, length us, event | category | flops | bytes accessed | tf_op | source)
XLA Modules:
  0.0 96.3 jit_solution(14746891240408900284)
XLA Ops:
  0.6 94.0 %shard_map.94 = (bf16[2,32,2048]{2,1,0:T(8,128)(2,1)}, f32[1,2048]{1,0:T(1,128)}) custom-call(bf16[32,2048]{1,0:T(8,128)(2,1)} %tok.1, s32[16,4,8,2048]{3,2,1,0:T(8,128)} %bitcast.4, s32[16,4,8,2048]{3,2,1,0:T(8,128)} %bitcast.5, s32[64,512]{1,0:T(8,128)} %bitcast.6, bf16[2048,896]{1,0:T(8,128)(2,1)} %wg_hbm.1, bf16[2048,896]{1,0:T(8,128)(2,1)} %wu_hbm.1, ...), custom_call_target="tpu_custom_call" | custom-call | tf_op jit(solution)/shard_map/pallas_call | solution.py:508
  94.7 1.7 %shard_map.95 = (bf16[32,2048]{1,0:T(8,128)(2,1)}, bf16[32,2048]{1,0:T(8,128)(2,1)}, f32[2048]{0:T(1024)}) custom-call(bf16[2,32,2048]{2,1,0:T(8,128)(2,1)} %get-tuple-element.5.total, f32[2048]{0:T(1024)} %bitcast.7), custom_call_target="tpu_custom_call" | custom-call | tf_op jit(solution)/shard_map/pallas_call | solution.py:568

commit v6 on v4

--- a/solution.py
+++ b/solution.py
@@ -254,7 +254,6 @@
     enter_second()
     own_tok(across).start()
     own_tok((2, 0)).start()
-    fold(0, 0)
 
     @pl.loop(0, NCH)
     def _(s):
@@ -262,6 +261,7 @@
 
         @pl.when(s == 0)
         def _():
+            fold(0, 0)
             fold(0, 1)
 
         @pl.when(s == 1)

time: 96.4 us -> 96.7 us (level)
  no operation moved by 1% of the time
where the time goes in v6:
time: 96.7 us; the launch traced here: 96.5 us
  Pallas kernels  95.9 us (99%)
    pallas_call x1, Pallas kernels, local(): pl.pallas_call(kernel, out_shape=(jax.ShapeDtypeStruct((2, NCH * SUB, FE)...  94.2 us

profile of v6, /device:TPU:0, one launch (start us, length us, event | category | flops | bytes accessed | tf_op | source)
XLA Modules:
  0.0 96.5 jit_solution(17674438553575030985)
XLA Ops:
  0.6 94.2 %shard_map.94 = (bf16[2,32,2048]{2,1,0:T(8,128)(2,1)}, f32[1,2048]{1,0:T(1,128)}) custom-call(bf16[32,2048]{1,0:T(8,128)(2,1)} %tok.1, s32[16,4,8,2048]{3,2,1,0:T(8,128)} %bitcast.4, s32[16,4,8,2048]{3,2,1,0:T(8,128)} %bitcast.5, s32[64,512]{1,0:T(8,128)} %bitcast.6, bf16[2048,896]{1,0:T(8,128)(2,1)} %wg_hbm.1, bf16[2048,896]{1,0:T(8,128)(2,1)} %wu_hbm.1, ...), custom_call_target="tpu_custom_call" | custom-call | tf_op jit(solution)/shard_map/pallas_call | solution.py:484
  94.9 1.7 %shard_map.95 = (bf16[32,2048]{1,0:T(8,128)(2,1)}, bf16[32,2048]{1,0:T(8,128)(2,1)}, f32[2048]{0:T(1024)}) custom-call(bf16[2,32,2048]{2,1,0:T(8,128)(2,1)} %get-tuple-element.5.total, f32[2048]{0:T(1024)} %bitcast.7), custom_call_target="tpu_custom_call" | custom-call | tf_op jit(solution)/shard_map/pallas_call | solution.py:544
